TPU v7x, 256 devices: a whole 4x4x8 slice. The times are simulated.
256 devices in a mesh: cam: 8 (over x, z_lo), pts: 32 (over y, z_hi, core).
Axes of the slice: x: 4, y: 4, z: 8 (z_hi: 4, z_lo: 2; z = z_hi * 2 + z_lo), core: 2. Of those that a mesh axis runs over, the one named last changes fastest.
Arguments:
- cam_jac: bfloat16 [12, 131072], P(None, ('cam', 'pts')), may hold values from -3 to 3
- pt_jac: bfloat16 [6, 131072], P(None, ('cam', 'pts')), may hold values from -6 to 6
- resid: float32 [2, 131072], P(None, ('cam', 'pts')), may hold values from -0.6 to 0.6
- obs_cam: int32 [131072], P(('cam', 'pts')), may hold values from 0 to 255, as said below
- obs_pt: int32 [131072], P(('cam', 'pts')), may hold values from 0 to 4095, as said below
- pairs: int32 [2, 16384], P(None, ('cam', 'pts')), may hold values from 0 to 255, as said below
- damping: float32 [1], replicated, may hold values from 1 to 8
Outputs:
- schur_blocks: float32 [36, 16384], P(None, ('cam', 'pts'))
- reduced_rhs: float32 [6, 256], P(None, 'cam')
Inputs may be any that keep to these rules, and one draw needn't show every extreme that they name: `obs_cam`: observation block number g * 32 + b (aligned blocks of 512) holds only cameras g * 32 to (g + 1) * 32 - 1 and points b * 128 to (b + 1) * 128 - 1; no camera observes a point twice. `obs_pt`: see obs_cam: within aligned block g * 32 + b the points lie in range b. In aligned block g * 32 + b of 64 pairs, pairs[0] lies in cameras g * 32 to (g + 1) * 32 - 1 and pairs[1] in cameras b * 8 to (b + 1) * 8 - 1; pairs may repeat.
All inputs are finite; a program needn't handle non-finite values.
Results may differ from a plain program's by a relative error of at most 0.0016.
Values may be sent and summed in bfloat16 or wider, within the bound.
No kernel may reach another device: no remote copies, remote signals or barrier semaphores. Data moves between devices by JAX's collectives and lax.ppermute only.
A program may use at most 64 MiB of HBM per device.

v0:
```python
import jax
import jax.numpy as jnp
from jax import lax
from jax.sharding import PartitionSpec as P

CAM_DEV = 32
PT_DEV = 128


def point_parts(pt_jac, resid):
    jp = pt_jac.astype(jnp.float32)

    def entry(s, t):
        return jp[s] * jp[t] + jp[3 + s] * jp[3 + t]

    grads = [jp[s] * resid[0] + jp[3 + s] * resid[1] for s in range(3)]
    return jnp.stack(
        [entry(0, 0), entry(0, 1), entry(0, 2), entry(1, 1), entry(1, 2), entry(2, 2)] + grads
    )


def invert(stats, lam):
    a = stats[0] + lam
    b = stats[1]
    c = stats[2]
    d = stats[3] + lam
    e = stats[4]
    f = stats[5] + lam
    m00 = d * f - e * e
    m01 = c * e - b * f
    m02 = b * e - c * d
    m11 = a * f - c * c
    m12 = b * c - a * e
    m22 = a * d - b * b
    det = a * m00 + b * m01 + c * m02
    return jnp.stack([m00, m01, m02, m11, m12, m22]) / det


def full_inverse(inv):
    return [[inv[0], inv[1], inv[2]], [inv[1], inv[3], inv[4]], [inv[2], inv[4], inv[5]]]


def solve_point(inv, grads):
    full = full_inverse(inv)
    return jnp.stack(
        [full[r][0] * grads[0] + full[r][1] * grads[1] + full[r][2] * grads[2] for r in range(3)]
    )


def couple(cam_jac, pt_jac):
    jc = cam_jac.astype(jnp.float32)
    jp = pt_jac.astype(jnp.float32)
    return jnp.stack([jc[k] * jp[s] + jc[6 + k] * jp[3 + s] for k in range(6) for s in range(3)])


def camera_terms(cam_jac, resid, coupling, y_obs):
    jc = cam_jac.astype(jnp.float32)
    rows = []
    for k in range(6):
        value = jc[k] * resid[0] + jc[6 + k] * resid[1]
        value = value - (
            coupling[k * 3] * y_obs[0]
            + coupling[k * 3 + 1] * y_obs[1]
            + coupling[k * 3 + 2] * y_obs[2]
        )
        rows.append(value)
    return jnp.stack(rows)


def scale_obs(rounded, inv_obs):
    full = full_inverse(inv_obs)
    return jnp.stack(
        [
            rounded[k * 3] * full[0][t]
            + rounded[k * 3 + 1] * full[1][t]
            + rounded[k * 3 + 2] * full[2][t]
            for k in range(6)
            for t in range(3)
        ]
    )


def place(values, cams, points, ncams, npoints):
    count = values.shape[1]
    cam_hot = (cams[None, :] == jnp.arange(ncams, dtype=jnp.int32)[:, None]).astype(jnp.bfloat16)
    pt_hot = (points[:, None] == jnp.arange(npoints, dtype=jnp.int32)[None, :]).astype(jnp.bfloat16)
    spread = (cam_hot[None, :, :] * values.reshape(18, 1, count)).reshape(18 * ncams, count)
    grid = lax.dot_general(
        spread, pt_hot, (((1,), (0,)), ((), ())), preferred_element_type=jnp.float32
    )
    grid = grid.reshape(6, 3, ncams, npoints).transpose(2, 0, 1, 3).reshape(ncams * 6, 3 * npoints)
    return grid.astype(jnp.bfloat16)


def against(weighted, design):
    return lax.dot_general(
        weighted, design, (((1,), (1,)), ((), ())), preferred_element_type=jnp.float32
    )


def pick_blocks(matrix, left, right):
    row_count = matrix.shape[0] // 6
    col_count = matrix.shape[1] // 6
    blocked = (
        matrix.reshape(row_count, 6, col_count, 6)
        .transpose(0, 2, 1, 3)
        .reshape(row_count * col_count, 36)
    )
    return blocked[left * col_count + right]


def local(cam_jac, pt_jac, resid, obs_cam, obs_pt, pairs, damping):
    groups = lax.axis_size("cam")
    group = lax.axis_index("cam")
    block = lax.axis_index("pts")
    ncams = CAM_DEV * groups
    lam = damping[0]
    local_pt = obs_pt - block * PT_DEV
    local_cam = obs_cam - group * CAM_DEV
    stats = point_parts(pt_jac, resid)
    partial_stats = jnp.zeros((9, PT_DEV), jnp.float32).at[:, local_pt].add(stats)
    totals = lax.psum(partial_stats, "cam")
    inv = invert(totals, lam)
    y_pts = solve_point(inv, totals[6:])
    coupling = couple(cam_jac, pt_jac)
    inv_obs = inv[:, local_pt]
    y_obs = y_pts[:, local_pt]
    terms = camera_terms(cam_jac, resid, coupling, y_obs)
    rhs_part = jnp.zeros((6, CAM_DEV), jnp.float32).at[:, local_cam].add(terms)
    reduced_rhs = lax.psum(rhs_part, "pts")
    rounded = coupling.astype(jnp.bfloat16)
    scaled = scale_obs(rounded.astype(jnp.float32), inv_obs).astype(jnp.bfloat16)
    weighted = place(scaled, local_cam, local_pt, CAM_DEV, PT_DEV)
    codes = (obs_cam * PT_DEV + local_pt)[None, :]
    shared_vals, shared_codes = (
        lax.all_gather(rounded, "cam", axis=1, tiled=True),
        lax.all_gather(codes, "cam", axis=1, tiled=True),
    )
    design = place(shared_vals, shared_codes[0] // PT_DEV, shared_codes[0] % PT_DEV, ncams, PT_DEV)
    partial_value = against(weighted, design)
    every = lax.all_gather(pairs, "pts", axis=1, tiled=True)
    schur_blocks = lax.psum_scatter(
        pick_blocks(partial_value, every[0] - group * CAM_DEV, every[1]),
        "pts",
        scatter_dimension=0,
        tiled=True,
    ).T
    return (schur_blocks, reduced_rhs)


def solution(mesh):
    return jax.shard_map(
        local,
        mesh=mesh,
        in_specs=(
            P(None, ("cam", "pts")),
            P(None, ("cam", "pts")),
            P(None, ("cam", "pts")),
            P(("cam", "pts")),
            P(("cam", "pts")),
            P(None, ("cam", "pts")),
            P(),
        ),
        out_specs=(P(None, ("cam", "pts")), P(None, "cam")),
        check_vma=False,
    )
```

profile of v0, /device:TPU:1, one launch (start us, length us, event | category | flops | bytes accessed | tf_op | source)
XLA Modules:
  0.0 322.2 jit_solution(18042928577674585108)
XLA Ops:
  7.9 0.7 compare_select_fusion.5
  8.6 0.7 convert_element_type.54
  9.3 0.8 multiply_add_fusion.1
  10.3 2.3 scatter_custom_fusion
  12.6 17.6 %psum.14 = f32[9,128]{1,0:T(8,128)S(1)} all-reduce(f32[9,128]{1,0:T(8,128)S(1)} %copy.379), channel_id=1, replica_groups=mesh['cam'=8,'pts'=32] {'cam'}, use_global_device_ids=true, to_apply=%region_1.0 | all-reduce | flops 1152 | bytes 9216 | tf_op jit(solution)/shard_map/psum | solution.py:122
  30.4 0.7 convert_element_type.53
  31.2 1.0 gather_fusion.2
  32.4 0.8 add_subtract_fusion.2
  33.2 0.8 add_subtract_fusion.1
  34.0 0.8 add_subtract_fusion
  34.8 1.4 add_subtract_fusion.4
  36.1 1.4 add_subtract_fusion.3
  37.5 1.4 add_subtract_fusion.5
  39.1 22.8 %all_gather.10 = bf16[18,4096]{1,0:T(8,128)(2,1)S(1)} all-gather(bf16[18,512]{1,0:T(8,128)(2,1)S(1)} %stack.49), channel_id=1, replica_groups=mesh['cam'=8,'pts'=32] {'cam'}, dimensions={1}, use_global_device_ids=true | all-gather | bytes 165888 | tf_op jit(solution)/shard_map/all_gather | solution.py:136
  61.9 1.0 gather_fusion
  63.0 1.3 fusion.42
  64.2 1.0 fusion.41
  65.2 1.0 fusion.39
  66.2 1.1 fusion.47
  67.3 1.0 fusion.48
  68.3 0.8 fusion.33
  69.6 19.1 %all-gather.1 = s32[8,1,512]{2,1,0:T(1,128)S(1)} all-gather(s32[1,1,512]{2,1,0:T(1,128)S(1)} %bitcast.86), channel_id=2, replica_groups=mesh['cam'=8,'pts'=32] {'cam'}, dimensions={0}, use_global_device_ids=true | all-gather | bytes 18432 | tf_op jit(solution)/shard_map/all_gather | solution.py:137
  89.4 62.3 %all-gather.2 = s32[32,64,2]{1,2,0:T(2,128)S(1)} all-gather(s32[1,64,2]{1,2,0:T(2,128)S(1)} %bitcast.87), channel_id=1, replica_groups=mesh['cam'=8,'pts'=32] {'pts'}, dimensions={0}, use_global_device_ids=true | all-gather | bytes 16896 | tf_op jit(solution)/shard_map/all_gather | solution.py:141
  152.8 10.8 %fusion.12 = bf16[256,6,3,128,1]{3,0,2,1,4:T(8,128)(2,1)S(1)} fusion(bf16[6,3,4096]{2,1,0:T(4,128)(2,1)S(1)} %mul.876, bf16[256,4096]{1,0:T(8,128)(2,1)S(1)} %fusion.4, s32[4096]{0:T(1024)} %add_select_fusion), kind=kOutput, calls=%fused_computation.14 | convolution fusion | flops 4851826688 | bytes 3440640 | tf_op jit(solution)/shard_map/dot_general | solution.py:88
  163.6 1.1 fusion.19
  164.9 1.0 copy.393
  165.9 2.7 copy.382
  168.6 9.8 %gather_fusion.1 = f32[2048,36]{1,0:T(8,128)} fusion(f32[8192,36]{1,0:T(8,128)} %copy.382, s32[2048]{0:T(1024)S(1)} %broadcast_clamp_fusion), kind=kCustom, calls=%fused_computation.1 | custom fusion | bytes 598016 | tf_op jit(solution)/shard_map/gather | solution.py:109
  178.6 2.4 scatter_custom_fusion.1
  181.0 132.2 %psum.15 = f32[6,32]{0,1:T(8,128)S(1)} all-reduce(f32[6,32]{0,1:T(8,128)S(1)} %scatter_custom_fusion.1), channel_id=1, replica_groups=mesh['cam'=8,'pts'=32] {'pts'}, use_global_device_ids=true, to_apply=%region_4.5 | all-reduce | flops 192 | bytes 1536 | tf_op jit(solution)/shard_map/psum | solution.py:130
  313.3 0.7 copy.387
  313.9 1.4 copy.386
  (63 shorter events, 3.6 us)
Async XLA Ops:
  7.2 306.8 %reduce-scatter.2.cloned.1.call-start = ((), (), s32[]{:S(2)}) async-start(), calls=%async_computation.1 | async-start | bytes 1081344 | tf_op jit(solution)/shard_map/reduce_scatter | solution.py:142
  67.3 1.8 copy-start.3
  67.3 22.2 %copy-start.4 = (s32[2,64]{1,0:T(2,128)S(1)}, s32[2,64]{1,0:T(2,128)}, u32[]{:S(2)}) copy-start(s32[2,64]{1,0:T(2,128)} %param.12) | copy-start | bytes 1540
  168.6 9.8 %copy-start = (f32[1,512]{1,0:T(1,128)S(1)}, f32[1,512]{1,0:T(1,128)}, u32[]{:S(2)}) copy-start(f32[1,512]{1,0:T(1,128)} %get-tuple-element.48) | copy-start | bytes 6148
  168.6 9.8 %copy-start.1 = (f32[1,512]{1,0:T(1,128)S(1)}, f32[1,512]{1,0:T(1,128)}, u32[]{:S(2)}) copy-start(f32[1,512]{1,0:T(1,128)} %get-tuple-element.44) | copy-start | bytes 6148
  168.6 9.8 %copy-start.2 = (f32[1,512]{1,0:T(1,128)S(1)}, f32[1,512]{1,0:T(1,128)}, u32[]{:S(2)}) copy-start(f32[1,512]{1,0:T(1,128)} %get-tuple-element.52) | copy-start | bytes 6148
Sparse Core Ops, SparseCore 0:
  178.5 78.6 reduce-scatter.1
where the time goes:
time: 327 us; the launch traced here: 322 us
  blocking collectives  254 us (78%)
  other arithmetic  22 us (7%)
  local copies, waits for them, and re-layouts  19.3 us (6%)
  between operations  15 us (5%)
  matrix products  11.9 us (4%)
    psum x1, blocking collectives, local(): reduced_rhs = lax.psum(rhs_part, 'pts')  132 us
    all_gather x1, blocking collectives, local(): every = lax.all_gather(pairs, 'pts', axis=1, tiled=True)  62.3 us
    all_gather x1, blocking collectives, local(): lax.all_gather(rounded, 'cam', axis=1, tiled=True)  22.8 us
    all_gather x1, blocking collectives, local(): lax.all_gather(codes, 'cam', axis=1, tiled=True)  19.1 us
    psum x1, blocking collectives, local(): totals = lax.psum(partial_stats, 'cam')  17.6 us
    dot_general x1, matrix products, place(): lax.dot_general(spread, pt_hot, (((1,), (0,)), ((), ())), preferred_eleme...  10.8 us
    gather x1, local copies, waits for them, and re-layouts, pick_blocks(): return blocked[left * col_count + right]  9.78 us
  transfers between devices with their start and end apart: 1, of which 0 were waited for; matrix products, arithmetic and copies ran while one was open for 1% of the time, Pallas kernels for 0%

commit v1 on v0

v1 whole, which is shorter than its diff:
```python
import jax
import jax.numpy as jnp
from jax import lax
from jax.experimental import pallas as pl
from jax.experimental.pallas import tpu as pltpu
from jax.sharding import PartitionSpec as P

CAM_DEV = 32
PT_DEV = 128
OBS_DEV = 512
PAIR_DEV = 64
N_CAM = 8
N_PTS = 32
SLICE = 8
ROWS = 80
F32 = jnp.float32
BF16 = jnp.bfloat16


def split3(x):
    hi = x.astype(BF16)
    rest = x - hi.astype(F32)
    mid = rest.astype(BF16)
    low = (rest - mid.astype(F32)).astype(BF16)
    return hi.astype(F32), mid.astype(F32), low.astype(F32)


def nt(a, b):
    return lax.dot_general(a, b, (((1,), (1,)), ((), ())), preferred_element_type=F32)


def nn(a, b):
    return lax.dot_general(a, b, (((1,), (0,)), ((), ())), preferred_element_type=F32)


def pack_kernel(cj_ref, pj_ref, res_ref, cam_ref, pt_ref, out_ref):
    cj = cj_ref[...].astype(F32)
    pj = pj_ref[...].astype(F32)
    res = res_ref[...]
    high = res.astype(BF16).astype(F32)
    low = res - high
    cam = (cam_ref[...] & (CAM_DEV - 1)).astype(F32)
    pt = (pt_ref[...] & (PT_DEV - 1)).astype(F32)
    left = jnp.concatenate([cj[:6], high, cj[6:], low], axis=0).astype(BF16)
    right = jnp.concatenate([pj, cam, pt], axis=0)
    right = jnp.concatenate([right[:, :256], right[:, 256:]], axis=0).astype(BF16)
    for g in range(N_CAM):
        out_ref[g, :, :OBS_DEV] = left
        out_ref[g, :, OBS_DEV:] = right


def unpack(m):
    x = m[:, :OBS_DEV].astype(F32)
    y = m[:, OBS_DEV:].astype(F32)
    return x[:8], x[8:], jnp.concatenate([y[:8], y[8:]], axis=1)


def spread(x0, x1, pj, hots):
    blocks = []
    for s in range(3):
        e = x0 * pj[s : s + 1] + x1 * pj[3 + s : 4 + s]
        for hot in hots:
            for k in range(6):
                blocks.append(hot * e[k : k + 1])
    return blocks


def main_kernel(ranges, subs, id_ref, lam_ref, *refs):
    gat_refs = refs[:ranges]
    out_ref, d_ref, w_ref = refs[ranges:]
    group = id_ref[0]
    core = id_ref[1]
    lam = lam_ref[0]
    iota8 = lax.broadcasted_iota(jnp.int32, (8, OBS_DEV), 0)
    iota32 = lax.broadcasted_iota(jnp.int32, (CAM_DEV, OBS_DEV), 0).astype(F32)
    iotap = lax.broadcasted_iota(jnp.int32, (PT_DEV, OBS_DEV), 0).astype(F32)
    step = 4 // subs
    firsts = [(iota8 + ((h * step + core) if subs < 4 else h) * SLICE).astype(F32) for h in range(subs)]
    per = subs * 48
    rhs = jnp.zeros((8, CAM_DEV), F32)

    for r in range(ranges):
        gat_ref = gat_refs[r]

        def one_group(g, totals):
            x0, x1, pj = unpack(gat_ref[g])
            cam = pj[6:7]
            pt = pj[7:8]
            hots = [jnp.where(f == cam, 1.0, 0.0) for f in firsts]
            blocks = spread(x0, x1, pj, hots)
            res = x0 + x1
            jp = [pj[i : i + 1] for i in range(6)]
            r0 = res[6:7]
            r1 = res[7:8]
            stats = [jp[s] * jp[t] + jp[3 + s] * jp[3 + t] for s, t in
                     ((0, 0), (0, 1), (0, 2), (1, 1), (1, 2), (2, 2))]
            stats = stats + [jp[s] * r0 + jp[3 + s] * r1 for s in range(3)]
            stats = stats + [jnp.zeros((7, OBS_DEV), F32)]
            rows = jnp.concatenate(stats, axis=0)
            left = jnp.concatenate(blocks + list(split3(rows)), axis=0).astype(BF16)
            pt_hot = jnp.where(iotap == pt, 1.0, 0.0).astype(BF16)
            grid = nt(left, pt_hot)
            for s in range(3):
                at = (r * 3 + s) * PT_DEV
                d_ref[g, :, at : at + PT_DEV] = grid[s * per : (s + 1) * per].astype(BF16)
            top = 3 * per
            return totals + (grid[top : top + 16] + grid[top + 16 : top + 32] + grid[top + 32 : top + 48])

        totals = lax.fori_loop(0, N_CAM, one_group, jnp.zeros((16, PT_DEV), F32))

        a = totals[0:1] + lam
        b = totals[1:2]
        c = totals[2:3]
        d = totals[3:4] + lam
        e = totals[4:5]
        f = totals[5:6] + lam
        m00 = d * f - e * e
        m01 = c * e - b * f
        m02 = b * e - c * d
        m11 = a * f - c * c
        m12 = b * c - a * e
        m22 = a * d - b * b
        det = a * m00 + b * m01 + c * m02
        i00, i01, i02, i11, i12, i22 = [m / det for m in (m00, m01, m02, m11, m12, m22)]
        full = [[i00, i01, i02], [i01, i11, i12], [i02, i12, i22]]
        grads = [totals[6 + s : 7 + s] for s in range(3)]
        y = [full[q][0] * grads[0] + full[q][1] * grads[1] + full[q][2] * grads[2] for q in range(3)]

        x0, x1, pj = unpack(gat_ref[group])
        cam = pj[6:7]
        pt = pj[7:8]
        cam_hot = jnp.where(iota32 == cam, 1.0, 0.0)
        pt_hot = jnp.where(iotap == pt, 1.0, 0.0).astype(BF16)
        left = jnp.concatenate(spread(x0, x1, pj, [cam_hot]), axis=0).astype(BF16)
        grid = nt(left, pt_hot)
        for t in range(3):
            value = grid[:192] * full[0][t] + grid[192:384] * full[1][t] + grid[384:] * full[2][t]
            at = (r * 3 + t) * PT_DEV
            w_ref[:, at : at + PT_DEV] = value.astype(BF16)

        y8 = jnp.concatenate(y + [jnp.zeros((5, PT_DEV), F32)], axis=0)
        y_obs = nn(jnp.concatenate(split3(y8), axis=0).astype(BF16), pt_hot)
        y_obs = y_obs[:8] + y_obs[8:16] + y_obs[16:24]
        res = x0 + x1
        left0 = res[6:7] - (pj[0:1] * y_obs[0:1] + pj[1:2] * y_obs[1:2] + pj[2:3] * y_obs[2:3])
        left1 = res[7:8] - (pj[3:4] * y_obs[0:1] + pj[4:5] * y_obs[1:2] + pj[5:6] * y_obs[2:3])
        terms = x0 * left0 + x1 * left1
        part = nt(jnp.concatenate(split3(terms), axis=0).astype(BF16), cam_hot.astype(BF16))
        rhs = rhs + (part[:8] + part[8:16] + part[16:24])

    rhs_high = rhs.astype(BF16).astype(F32)
    rhs_rows = jnp.concatenate([rhs_high, rhs - rhs_high, jnp.zeros((8, 64), F32)], axis=1)
    w = w_ref[...]

    def one_product(g, carry):
        product = nt(d_ref[g], w)
        for h in range(subs):
            block = product[h * 48 : (h + 1) * 48]
            tail = block[:, 128:192]
            tail = jnp.concatenate([tail[:24], tail[24:]], axis=1)
            whole = jnp.concatenate([block[:, :128], tail, rhs_rows], axis=0)
            out_ref[g * subs + h] = whole.astype(BF16)
        return carry

    lax.fori_loop(0, N_CAM, one_product, 0)


def last_kernel(got_ref, pairs_ref, schur_ref, rhs_ref):
    total = got_ref[0].astype(F32)
    for i in range(1, got_ref.shape[0]):
        total = total + got_ref[i].astype(F32)
    rhs = total[72:80]
    rhs_ref[...] = rhs[:6, :CAM_DEV] + rhs[:6, CAM_DEV : 2 * CAM_DEV]
    tail = total[48:72]
    tail = jnp.concatenate([tail[:, :64], tail[:, 64:]], axis=0)
    tail = jnp.concatenate([tail, jnp.zeros((48, 64), F32)], axis=1)
    pairs = pairs_ref[...]
    left = (pairs[0:1] & (CAM_DEV - 1))
    right = (pairs[1:2] & (SLICE - 1))
    lefts = jnp.concatenate([left + CAM_DEV * k for k in range(4)], axis=1)
    rights = jnp.concatenate([right] * 6, axis=1)
    pick = jnp.where(
        lax.broadcasted_iota(jnp.int32, (128, 256), 0) == lefts, 1.0, 0.0
    ).astype(BF16)
    first = nn(jnp.concatenate(split3(total[:48]), axis=0).astype(BF16), pick)
    second = nn(jnp.concatenate(split3(tail), axis=0).astype(BF16), pick[:, :128])
    z = jnp.concatenate([first, second], axis=1)
    z = z[:48] + z[48:96] + z[96:]
    keep = lax.broadcasted_iota(jnp.int32, (SLICE, 384), 0) == rights
    rows = [
        jnp.sum(jnp.where(keep, z[l * 8 : (l + 1) * 8], 0.0), axis=0, keepdims=True) for l in range(6)
    ]
    rows = jnp.concatenate(rows, axis=0)
    for k in range(6):
        schur_ref[k * 6 : (k + 1) * 6, :] = rows[:, k * PAIR_DEV : (k + 1) * PAIR_DEV]


def local(cam_jac, pt_jac, resid, obs_cam, obs_pt, pairs, damping):
    group = lax.axis_index("cam")
    block = lax.axis_index("pts")
    smem = pl.BlockSpec(memory_space=pltpu.SMEM)
    vmem = pl.BlockSpec(memory_space=pltpu.VMEM)
    packed = pl.pallas_call(
        pack_kernel,
        out_shape=jax.ShapeDtypeStruct((N_CAM, 16, 768), BF16),
        in_specs=[vmem] * 5,
        out_specs=vmem,
    )(cam_jac, pt_jac, resid, obs_cam.reshape(1, OBS_DEV), obs_pt.reshape(1, OBS_DEV))
    gathered = lax.all_to_all(packed, "cam", 0, 0)
    ids = jnp.stack([group, block % 2]).astype(jnp.int32)
    if MERGE:
        other = lax.ppermute(gathered, "pts", [(i, i ^ 1) for i in range(N_PTS)])
        gats = [gathered, other]
        ranges, subs = 2, 2
    else:
        gats = [gathered]
        ranges, subs = 1, 4
    sends = N_CAM * subs
    send = pl.pallas_call(
        lambda *refs: main_kernel(ranges, subs, *refs),
        out_shape=jax.ShapeDtypeStruct((sends, ROWS, 128), BF16),
        in_specs=[smem, smem] + [vmem] * ranges,
        out_specs=vmem,
        scratch_shapes=[
            pltpu.VMEM((N_CAM, subs * 48, ranges * 3 * PT_DEV), BF16),
            pltpu.VMEM((192, ranges * 3 * PT_DEV), BF16),
        ],
    )(ids, damping, *gats)
    if MERGE:
        same = [[2 * i + c for i in range(N_PTS // 2)] for c in range(2)]
        got = lax.all_to_all(send, "pts", 0, 0, axis_index_groups=same)
    else:
        got = lax.all_to_all(send, "pts", 0, 0)
    return pl.pallas_call(
        last_kernel,
        out_shape=(
            jax.ShapeDtypeStruct((36, PAIR_DEV), F32),
            jax.ShapeDtypeStruct((6, CAM_DEV), F32),
        ),
        in_specs=[vmem, vmem],
        out_specs=(vmem, vmem),
    )(got, pairs)


MERGE = False


def solution(mesh):
    return jax.shard_map(
        local,
        mesh=mesh,
        in_specs=(
            P(None, ("cam", "pts")),
            P(None, ("cam", "pts")),
            P(None, ("cam", "pts")),
            P(("cam", "pts")),
            P(("cam", "pts")),
            P(None, ("cam", "pts")),
            P(),
        ),
        out_specs=(P(None, ("cam", "pts")), P(None, "cam")),
        check_vma=False,
    )
```

time: 327 us -> 57.9 us (0.18); the launches traced: 322 us -> 57.5 us
  blocking collectives: 254 us -> 33.2 us
  other arithmetic: 22 us -> 0.65 us
  local copies, waits for them, and re-layouts: 19.3 us -> 0.68 us
  between operations: 15 us -> 1.29 us
  matrix products: 11.9 us -> 0 us
  Pallas kernels: 0 us -> 11 us
  starting transfers between devices: 0.04 us -> 6.2 us
  waiting for transfers between devices: 0.02 us -> 4.61 us
    psum x2 -> x0, blocking collectives: 150 us -> none  [the longest x1 132 us: local(): reduced_rhs = lax.psum(rhs_part, 'pts')]
    all_gather x3 -> x0, blocking collectives: 104 us -> none  [the longest x1 62.3 us: local(): every = lax.all_gather(pairs, 'pts', axis=1, tiled=True)]
    all_to_all x0 -> x1, blocking collectives: none -> 33.2 us  [local(): got = lax.all_to_all(send, 'pts', 0, 0)]
    gather x4 -> x0, local copies, waits for them, and re-layouts: 11.9 us -> none  [the longest x1 9.78 us: pick_blocks(): return blocked[left * col_count + right]]
    dot_general x2 -> x0, matrix products: 11.9 us -> none  [the longest x1 10.8 us: place(): lax.dot_general(spread, pt_hot, (((1,), (0,)), ((), ())), preferred_eleme...]
    pallas_call x0 -> x3, Pallas kernels: none -> 11 us  [the longest x1 7.49 us: local(): pl.pallas_call(lambda *refs: main_kernel(ranges, subs, *refs), out_shape=...]
    sub x7 -> x0, other arithmetic: 6.49 us -> none  [the longest x6 6.48 us: camera_terms(): value - (coupling[k * 3] * y_obs[0] + coupling[k * 3 + 1] * y_obs[1] + co...]
    all_to_all x0 -> x1, starting transfers between devices: none -> 6.2 us  [local(): gathered = lax.all_to_all(packed, 'cam', 0, 0)]
  transfers between devices with their start and end apart: 1 -> 1, of which waited for: 0 -> 1; matrix products, arithmetic and copies ran while one was open for 1% -> 1% of each run, Pallas kernels for 0% -> 0%
where the time goes in v1:
time: 57.9 us; the launch traced here: 57.5 us
  blocking collectives  33.2 us (57%)
  Pallas kernels  11 us (19%)
  starting transfers between devices  6.2 us (11%)
  waiting for transfers between devices  4.61 us (8%)
  between operations  1.29 us (2%)
  local copies, waits for them, and re-layouts  0.68 us (1%)
  other arithmetic  0.65 us (1%)
    all_to_all x1, blocking collectives, local(): got = lax.all_to_all(send, 'pts', 0, 0)  33.2 us
    pallas_call x1, Pallas kernels, local(): pl.pallas_call(lambda *refs: main_kernel(ranges, subs, *refs), out_shape=...  7.49 us
    all_to_all x1, starting transfers between devices, local(): gathered = lax.all_to_all(packed, 'cam', 0, 0)  6.2 us
    all_to_all x1, waiting for transfers between devices, local(): gathered = lax.all_to_all(packed, 'cam', 0, 0)  4.61 us
    pallas_call x1, Pallas kernels, local(): pl.pallas_call(last_kernel, out_shape=(jax.ShapeDtypeStruct((36, PAIR_DEV...  2.04 us
    pallas_call x1, Pallas kernels, local(): pl.pallas_call(pack_kernel, out_shape=jax.ShapeDtypeStruct((N_CAM, 16, 76...  1.44 us
  transfers between devices with their start and end apart: 1, of which 1 were waited for; matrix products, arithmetic and copies ran while one was open for 1% of the time, Pallas kernels for 0%

profile of v1, /device:TPU:1, one launch (start us, length us, event | category | flops | bytes accessed | tf_op | source)
XLA Modules:
  0.0 57.5 jit_solution(7210247105630975302)
XLA Ops:
  0.6 1.4 %shard_map.86 = bf16[8,16,768]{2,1,0:T(8,128)(2,1)} custom-call(bf16[12,512]{1,0:T(8,128)(2,1)} %cj_ref.1, bf16[6,512]{1,0:T(8,128)(2,1)} %pj_ref.1, f32[2,512]{1,0:T(2,128)} %res_ref.1, s32[1,512]{1,0:T(1,128)} %bitcast.4, s32[1,512]{1,0:T(1,128)} %bitcast.5), custom_call_target="tpu_custom_call" | custom-call | tf_op jit(solution)/shard_map/pallas_call | solution.py:203
  2.1 6.2 %all-to-all-start = ((bf16[8,16,768]{2,1,0:T(8,128)(2,1)}), bf16[8,16,768]{2,1,0:T(8,128)(2,1)S(1)}, u32[]{:S(2)}, u32[]{:S(2)}) async-start(bf16[8,16,768]{2,1,0:T(8,128)(2,1)} %shard_map.86), calls=%async_computation | async-start | bytes 393216 | tf_op jit(solution)/shard_map/all_to_all | solution.py:209
  8.9 0.7 %pad_add_fusion.refs_0_ = s32[2]{0:T(128)} fusion(s32[1]{0:T(128)} %bitcast.1, s32[1]{0:T(128)} %bitcast), kind=kLoop, calls=%fused_computation | loop fusion | flops 2 | bytes 16 | tf_op jit(solution)/shard_map/stack | solution.py:210
  9.6 4.6 %all-to-all-done.refs_2_ = bf16[8,16,768]{2,1,0:T(8,128)(2,1)S(1)} async-done(((bf16[8,16,768]{2,1,0:T(8,128)(2,1)}), bf16[8,16,768]{2,1,0:T(8,128)(2,1)S(1)}, u32[]{:S(2)}, u32[]{:S(2)}) %all-to-all-start) | async-done | bytes 196640 | tf_op jit(solution)/shard_map/all_to_all | solution.py:209
  14.2 0.0 copy-start
  14.2 0.7 %copy-done = bf16[8,16,768]{2,1,0:T(8,128)(2,1)} copy-done((bf16[8,16,768]{2,1,0:T(8,128)(2,1)}, bf16[8,16,768]{2,1,0:T(8,128)(2,1)S(1)}, u32[]{:S(2)}) %copy-start) | copy-done | bytes 196632
  14.9 7.5 %shard_map.87 = bf16[32,80,128]{2,1,0:T(8,128)(2,1)} custom-call(s32[2]{0:T(128)} %pad_add_fusion.refs_0_, f32[1]{0:T(128)S(6)} %copy.9.refs_1_, bf16[8,16,768]{2,1,0:T(8,128)(2,1)} %copy-done), custom_call_target="tpu_custom_call" | custom-call | tf_op jit(solution)/shard_map/pallas_call | solution.py:219
  22.4 33.2 %all_to_all.10.got_ref = bf16[32,80,128]{2,1,0:T(8,128)(2,1)} all-to-all(bf16[32,80,128]{2,1,0:T(8,128)(2,1)} %shard_map.87), channel_id=1, replica_groups=mesh['cam'=8,'pts'=32] {'pts'}, dimensions={0} | all-to-all | bytes 1310720 | tf_op jit(solution)/shard_map/all_to_all | solution.py:233
  55.5 2.0 %shard_map.88 = (f32[36,64]{1,0:T(8,128)}, f32[6,32]{1,0:T(8,128)}) custom-call(bf16[32,80,128]{2,1,0:T(8,128)(2,1)} %all_to_all.10.got_ref, s32[2,64]{1,0:T(2,128)} %pairs_ref.1), custom_call_target="tpu_custom_call" | custom-call | tf_op jit(solution)/shard_map/pallas_call | solution.py:234
Async XLA Ops:
  2.1 12.1 %all-to-all-start = ((bf16[8,16,768]{2,1,0:T(8,128)(2,1)}), bf16[8,16,768]{2,1,0:T(8,128)(2,1)S(1)}, u32[]{:S(2)}, u32[]{:S(2)}) async-start(bf16[8,16,768]{2,1,0:T(8,128)(2,1)} %shard_map.86), calls=%async_computation | async-start | bytes 393216 | tf_op jit(solution)/shard_map/all_to_all | solution.py:209
  14.2 0.7 %copy-start = (bf16[8,16,768]{2,1,0:T(8,128)(2,1)}, bf16[8,16,768]{2,1,0:T(8,128)(2,1)S(1)}, u32[]{:S(2)}) copy-start(bf16[8,16,768]{2,1,0:T(8,128)(2,1)S(1)} %all-to-all-done.refs_2_) | copy-start | bytes 589828

commit v2 on v1

--- a/solution.py
+++ b/solution.py
@@ -65,12 +65,12 @@
     return blocks
 
 
-def main_kernel(ranges, subs, id_ref, lam_ref, *refs):
+def main_kernel(ranges, subs, lam_ref, *refs):
     gat_refs = refs[:ranges]
     out_ref, d_ref, w_ref = refs[ranges:]
-    group = id_ref[0]
-    core = id_ref[1]
-    lam = lam_ref[0]
+    group = lax.axis_index("cam")
+    core = lax.axis_index("pts") % 2
+    lam = lam_ref[...]
     iota8 = lax.broadcasted_iota(jnp.int32, (8, OBS_DEV), 0)
     iota32 = lax.broadcasted_iota(jnp.int32, (CAM_DEV, OBS_DEV), 0).astype(F32)
     iotap = lax.broadcasted_iota(jnp.int32, (PT_DEV, OBS_DEV), 0).astype(F32)
@@ -106,7 +106,7 @@
             top = 3 * per
             return totals + (grid[top : top + 16] + grid[top + 16 : top + 32] + grid[top + 32 : top + 48])
 
-        totals = lax.fori_loop(0, N_CAM, one_group, jnp.zeros((16, PT_DEV), F32))
+        totals = lax.fori_loop(0, N_CAM, one_group, jnp.zeros((16, PT_DEV), F32), unroll=4)
 
         a = totals[0:1] + lam
         b = totals[1:2]
@@ -162,7 +162,7 @@
             out_ref[g * subs + h] = whole.astype(BF16)
         return carry
 
-    lax.fori_loop(0, N_CAM, one_product, 0)
+    lax.fori_loop(0, N_CAM, one_product, 0, unroll=4)
 
 
 def last_kernel(got_ref, pairs_ref, schur_ref, rhs_ref):
@@ -196,9 +196,6 @@
 
 
 def local(cam_jac, pt_jac, resid, obs_cam, obs_pt, pairs, damping):
-    group = lax.axis_index("cam")
-    block = lax.axis_index("pts")
-    smem = pl.BlockSpec(memory_space=pltpu.SMEM)
     vmem = pl.BlockSpec(memory_space=pltpu.VMEM)
     packed = pl.pallas_call(
         pack_kernel,
@@ -207,7 +204,6 @@
         out_specs=vmem,
     )(cam_jac, pt_jac, resid, obs_cam.reshape(1, OBS_DEV), obs_pt.reshape(1, OBS_DEV))
     gathered = lax.all_to_all(packed, "cam", 0, 0)
-    ids = jnp.stack([group, block % 2]).astype(jnp.int32)
     if MERGE:
         other = lax.ppermute(gathered, "pts", [(i, i ^ 1) for i in range(N_PTS)])
         gats = [gathered, other]
@@ -219,13 +215,14 @@
     send = pl.pallas_call(
         lambda *refs: main_kernel(ranges, subs, *refs),
         out_shape=jax.ShapeDtypeStruct((sends, ROWS, 128), BF16),
-        in_specs=[smem, smem] + [vmem] * ranges,
+        in_specs=[vmem] + [vmem] * ranges,
         out_specs=vmem,
+        compiler_params=SMALL,
         scratch_shapes=[
             pltpu.VMEM((N_CAM, subs * 48, ranges * 3 * PT_DEV), BF16),
             pltpu.VMEM((192, ranges * 3 * PT_DEV), BF16),
         ],
-    )(ids, damping, *gats)
+    )(damping.reshape(1, 1), *gats)
     if MERGE:
         same = [[2 * i + c for i in range(N_PTS // 2)] for c in range(2)]
         got = lax.all_to_all(send, "pts", 0, 0, axis_index_groups=same)
@@ -239,10 +236,12 @@
         ),
         in_specs=[vmem, vmem],
         out_specs=(vmem, vmem),
+        compiler_params=SMALL,
     )(got, pairs)
 
 
-MERGE = False
+MERGE = True
+SMALL = pltpu.CompilerParams(vmem_limit_bytes=16 * 1024 * 1024)
 
 
 def solution(mesh):

time: 57.9 us -> 46.8 us (0.81)
  starting transfers between devices: 6.2 us -> 2 us
  waiting for transfers between devices: 4.61 us -> 0.42 us
  Pallas kernels: 11 us -> 6.95 us
  blocking collectives: 33.2 us -> 35.9 us
  local copies, waits for them, and re-layouts: 0.68 us -> 0.01 us
  other arithmetic: 0.65 us -> 0 us
    all_to_all x1 -> x0, starting transfers between devices: 6.2 us -> none  [local(): gathered = lax.all_to_all(packed, 'cam', 0, 0)]
    all_to_all x1 -> x0, waiting for transfers between devices: 4.61 us -> none  [local(): gathered = lax.all_to_all(packed, 'cam', 0, 0)]
    pallas_call x1, Pallas kernels: 7.49 us -> 4.56 us  [local(): pl.pallas_call(lambda *refs: main_kernel(ranges, subs, *refs), out_shape=...]
    all_to_all x1 -> x2, blocking collectives: 33.2 us -> 35.9 us  [the longest x1 23.8 us: local(): got = lax.all_to_all(send, 'pts', 0, 0, axis_index_groups=same)]
    ppermute x0 -> x1, starting transfers between devices: none -> 2 us  [local(): other = lax.ppermute(gathered, 'pts', [(i, i ^ 1) for i in range(N_PTS)])]
    pallas_call x1, Pallas kernels: 2.04 us -> 0.94 us  [local(): pl.pallas_call(last_kernel, out_shape=(jax.ShapeDtypeStruct((36, PAIR_DEV...]
    unnamed x2, local copies, waits for them, and re-layouts: 0.68 us -> 0.01 us
    another operation x1 -> x0, other arithmetic: 0.65 us -> none  [local(): ids = jnp.stack([group, block % 2]).astype(jnp.int32)]
  transfers between devices with their start and end apart: 1 -> 1, of which waited for: 1 -> 1; matrix products, arithmetic and copies ran while one was open for 1% -> 0% of each run, Pallas kernels for 0% -> 0%
where the time goes in v2:
time: 46.8 us; the launch traced here: 46.6 us
  blocking collectives  35.9 us (77%)
  Pallas kernels  6.95 us (15%)
  starting transfers between devices  2 us (4%)
  between operations  1.3 us (3%)
    all_to_all x1, blocking collectives, local(): got = lax.all_to_all(send, 'pts', 0, 0, axis_index_groups=same)  23.8 us
    all_to_all x1, blocking collectives, local(): gathered = lax.all_to_all(packed, 'cam', 0, 0)  12.1 us
    pallas_call x1, Pallas kernels, local(): pl.pallas_call(lambda *refs: main_kernel(ranges, subs, *refs), out_shape=...  4.56 us
    ppermute x1, starting transfers between devices, local(): other = lax.ppermute(gathered, 'pts', [(i, i ^ 1) for i in range(N_PTS)])  2 us
    pallas_call x1, Pallas kernels, local(): pl.pallas_call(pack_kernel, out_shape=jax.ShapeDtypeStruct((N_CAM, 16, 76...  1.44 us
    pallas_call x1, Pallas kernels, local(): pl.pallas_call(last_kernel, out_shape=(jax.ShapeDtypeStruct((36, PAIR_DEV...  0.94 us
  transfers between devices with their start and end apart: 1, of which 1 were waited for; matrix products, arithmetic and copies ran while one was open for 0% of the time, Pallas kernels for 0%

profile of v2, /device:TPU:1, one launch (start us, length us, event | category | flops | bytes accessed | tf_op | source)
XLA Modules:
  0.0 46.6 jit_solution(16065141248743222019)
XLA Ops:
  0.6 1.4 %shard_map.86 = bf16[8,16,768]{2,1,0:T(8,128)(2,1)} custom-call(bf16[12,512]{1,0:T(8,128)(2,1)} %cj_ref.1, bf16[6,512]{1,0:T(8,128)(2,1)} %pj_ref.1, f32[2,512]{1,0:T(2,128)} %res_ref.1, s32[1,512]{1,0:T(1,128)} %bitcast.4, s32[1,512]{1,0:T(1,128)} %bitcast.5), custom_call_target="tpu_custom_call" | custom-call | tf_op jit(solution)/shard_map/pallas_call | solution.py:200
  2.1 12.1 %all_to_all.10.refs_1_ = bf16[8,16,768]{2,1,0:T(8,128)(2,1)S(1)} all-to-all(bf16[8,16,768]{2,1,0:T(8,128)(2,1)} %shard_map.86), channel_id=1, replica_groups=mesh['cam'=8,'pts'=32] {'cam'}, dimensions={0} | all-to-all | bytes 393216 | tf_op jit(solution)/shard_map/all_to_all | solution.py:206
  14.2 2.0 %collective-permute-start = (bf16[8,16,768]{2,1,0:T(8,128)(2,1)S(1)}, bf16[8,16,768]{2,1,0:T(8,128)(2,1)S(1)}, u32[]{:S(2)}, u32[]{:S(2)}) collective-permute-start(bf16[8,16,768]{2,1,0:T(8,128)(2,1)S(1)} %all_to_all.10.refs_1_), channel_id=1, source_target_pairs={{0,1},{1,0},{2,3},{3,2},{4,5},{5,4},{6,7},{7,6},{8,9},{9,8},{10,11... | collective-permute-start | bytes 589832 | tf_op jit(solution)/shard_map/ppermute | solution.py:208
  16.8 0.4 collective-permute-done.refs_2_
  17.3 4.6 %shard_map.87 = bf16[16,80,128]{2,1,0:T(8,128)(2,1)S(1)} custom-call(f32[1,1]{1,0:T(1,128)} %bitcast.3.refs_0_, bf16[8,16,768]{2,1,0:T(8,128)(2,1)S(1)} %all_to_all.10.refs_1_, bf16[8,16,768]{2,1,0:T(8,128)(2,1)S(1)} %collective-permute-done.refs_2_), custom_call_target="tpu_custom_call" | custom-call | tf_op jit(solution)/shard_map/pallas_call | solution.py:215
  21.8 0.0 copy-start
  21.8 23.8 %all_to_all.11.got_ref = bf16[16,80,128]{2,1,0:T(8,128)(2,1)S(1)} all-to-all(bf16[16,80,128]{2,1,0:T(8,128)(2,1)S(1)} %shard_map.87), channel_id=1, replica_groups={{0,2,4,6,8,10,12,14,16,18,20,22,24,26,28,30},{1,3,5,7,9,11,13,15,17,19,..., dimensions={0} | all-to-all | bytes 655360 | tf_op jit(solution)/shard_map/all_to_all | solution.py:228
  45.6 0.0 copy-done
  45.6 0.9 %shard_map.88 = (f32[36,64]{1,0:T(8,128)}, f32[6,32]{1,0:T(8,128)}) custom-call(bf16[16,80,128]{2,1,0:T(8,128)(2,1)S(1)} %all_to_all.11.got_ref, s32[2,64]{1,0:T(2,128)S(1)} %copy-done), custom_call_target="tpu_custom_call" | custom-call | tf_op jit(solution)/shard_map/pallas_call | solution.py:231
Async XLA Ops:
  14.2 3.1 %collective-permute-start = (bf16[8,16,768]{2,1,0:T(8,128)(2,1)S(1)}, bf16[8,16,768]{2,1,0:T(8,128)(2,1)S(1)}, u32[]{:S(2)}, u32[]{:S(2)}) collective-permute-start(bf16[8,16,768]{2,1,0:T(8,128)(2,1)S(1)} %all_to_all.10.refs_1_), channel_id=1, source_target_pairs={{0,1},{1,0},{2,3},{3,2},{4,5},{5,4},{6,7},{7,6},{8,9},{9,8},{10,11... | collective-permute-start | bytes 589832 | tf_op jit(solution)/shard_map/ppermute | solution.py:208
  21.8 23.8 %copy-start = (s32[2,64]{1,0:T(2,128)S(1)}, s32[2,64]{1,0:T(2,128)}, u32[]{:S(2)}) copy-start(s32[2,64]{1,0:T(2,128)} %pairs_ref.1) | copy-start | bytes 1540

commit v3 on v2

v3 whole, which is shorter than its diff:
```python
import jax
import jax.numpy as jnp
from jax import lax
from jax.experimental import pallas as pl
from jax.experimental.pallas import tpu as pltpu
from jax.sharding import PartitionSpec as P

CAM_DEV = 32
PT_DEV = 128
OBS_DEV = 512
PAIR_DEV = 64
N_CAM = 8
N_PTS = 32
SLICE = 8
ROWS = 80
F32 = jnp.float32
BF16 = jnp.bfloat16
UNROLL = 4
SMALL = pltpu.CompilerParams(vmem_limit_bytes=16 * 1024 * 1024)
SCRATCH = [pltpu.VMEM((N_CAM, 96, 768), BF16), pltpu.VMEM((192, 768), BF16)]


def split3(x):
    hi = x.astype(BF16)
    rest = x - hi.astype(F32)
    mid = rest.astype(BF16)
    low = (rest - mid.astype(F32)).astype(BF16)
    return hi.astype(F32), mid.astype(F32), low.astype(F32)


def nt(a, b):
    return lax.dot_general(a, b, (((1,), (1,)), ((), ())), preferred_element_type=F32)


def nn(a, b):
    return lax.dot_general(a, b, (((1,), (0,)), ((), ())), preferred_element_type=F32)


def pack_kernel(cj_ref, pj_ref, res_ref, cam_ref, pt_ref, out_ref):
    cj = cj_ref[...].astype(F32)
    pj = pj_ref[...].astype(F32)
    res = res_ref[...]
    high = res.astype(BF16).astype(F32)
    low = res - high
    cam = (cam_ref[...] & (CAM_DEV - 1)).astype(F32)
    pt = (pt_ref[...] & (PT_DEV - 1)).astype(F32)
    left = jnp.concatenate([cj[:6], high, cj[6:], low], axis=0).astype(BF16)
    right = jnp.concatenate([pj, cam, pt], axis=0)
    right = jnp.concatenate([right[:, :256], right[:, 256:]], axis=0).astype(BF16)
    for g in range(N_CAM):
        out_ref[g, :, :OBS_DEV] = left
        out_ref[g, :, OBS_DEV:] = right


def unpack(m):
    x = m[:, :OBS_DEV].astype(F32)
    y = m[:, OBS_DEV:].astype(F32)
    return x[:8], x[8:], jnp.concatenate([y[:8], y[8:]], axis=1)


def spread(x0, x1, pj, hots):
    blocks = []
    for s in range(3):
        e = x0 * pj[s : s + 1] + x1 * pj[3 + s : 4 + s]
        for hot in hots:
            for k in range(6):
                blocks.append(hot * e[k : k + 1])
    return blocks


def stat_rows(x0, x1, pj):
    res = x0 + x1
    jp = [pj[i : i + 1] for i in range(6)]
    r0 = res[6:7]
    r1 = res[7:8]
    rows = [jp[s] * jp[t] + jp[3 + s] * jp[3 + t] for s, t in
            ((0, 0), (0, 1), (0, 2), (1, 1), (1, 2), (2, 2))]
    rows = rows + [jp[s] * r0 + jp[3 + s] * r1 for s in range(3)]
    last = jnp.concatenate(list(split3(rows[8])) + [jnp.zeros((5, OBS_DEV), F32)], axis=0)
    return list(split3(jnp.concatenate(rows[:8], axis=0))) + [last]


def point_inverse(totals, lam):
    a = totals[0] + lam
    b = totals[1]
    c = totals[2]
    d = totals[3] + lam
    e = totals[4]
    f = totals[5] + lam
    m00 = d * f - e * e
    m01 = c * e - b * f
    m02 = b * e - c * d
    m11 = a * f - c * c
    m12 = b * c - a * e
    m22 = a * d - b * b
    det = a * m00 + b * m01 + c * m02
    i00, i01, i02, i11, i12, i22 = [m / det for m in (m00, m01, m02, m11, m12, m22)]
    full = [[i00, i01, i02], [i01, i11, i12], [i02, i12, i22]]
    y = [full[q][0] * totals[6] + full[q][1] * totals[7] + full[q][2] * totals[8] for q in range(3)]
    return full, y


def main_kernel(lam_ref, gat0_ref, gat1_ref, out_ref, d_ref, w_ref):
    group = lax.axis_index("cam")
    core = lax.axis_index("pts") % 2
    gat_refs = (gat0_ref, gat1_ref)
    iota8 = lax.broadcasted_iota(jnp.int32, (SLICE, OBS_DEV), 0) + core * SLICE
    firsts = [(iota8 + h * 2 * SLICE).astype(F32) for h in range(2)]
    iota32 = lax.broadcasted_iota(jnp.int32, (CAM_DEV, OBS_DEV), 0).astype(F32)
    iotap = lax.broadcasted_iota(jnp.int32, (PT_DEV, OBS_DEV), 0).astype(F32)

    def one_group(g, totals):
        after = []
        for r in range(2):
            x0, x1, pj = unpack(gat_refs[r][g])
            hots = [jnp.where(f == pj[6:7], 1.0, 0.0) for f in firsts]
            left = spread(x0, x1, pj, hots) + stat_rows(x0, x1, pj)
            left = jnp.concatenate(left, axis=0).astype(BF16)
            pt_hot = jnp.where(iotap == pj[7:8], 1.0, 0.0).astype(BF16)
            grid = nt(left, pt_hot)
            for s in range(3):
                at = (r * 3 + s) * PT_DEV
                d_ref[g, :, at : at + PT_DEV] = grid[s * 96 : (s + 1) * 96].astype(BF16)
            after.append(totals[r] + grid[288:320])
        return tuple(after)

    zero = jnp.zeros((32, PT_DEV), F32)
    totals = lax.fori_loop(0, N_CAM, one_group, (zero, zero), unroll=UNROLL)
    totals = jnp.concatenate(totals, axis=1)
    eight = totals[:8] + totals[8:16] + totals[16:24]
    ninth = totals[24:25] + totals[25:26] + totals[26:27]
    full, y = point_inverse([eight[i : i + 1] for i in range(8)] + [ninth], lam_ref[...])

    rhs = jnp.zeros((8, CAM_DEV), F32)
    for r in range(2):
        mine = slice(r * PT_DEV, (r + 1) * PT_DEV)
        x0, x1, pj = unpack(gat_refs[r][group])
        cam_hot = jnp.where(iota32 == pj[6:7], 1.0, 0.0)
        pt_hot = jnp.where(iotap == pj[7:8], 1.0, 0.0).astype(BF16)
        left = jnp.concatenate(spread(x0, x1, pj, [cam_hot]), axis=0).astype(BF16)
        grid = nt(left, pt_hot)
        for t in range(3):
            value = (grid[:192] * full[0][t][:, mine] + grid[192:384] * full[1][t][:, mine]
                     + grid[384:] * full[2][t][:, mine])
            at = (r * 3 + t) * PT_DEV
            w_ref[:, at : at + PT_DEV] = value.astype(BF16)
        y8 = jnp.concatenate([v[:, mine] for v in y] + [jnp.zeros((5, PT_DEV), F32)], axis=0)
        y_obs = nn(jnp.concatenate(split3(y8), axis=0).astype(BF16), pt_hot)
        y_obs = y_obs[:8] + y_obs[8:16] + y_obs[16:24]
        res = x0 + x1
        left0 = res[6:7] - (pj[0:1] * y_obs[0:1] + pj[1:2] * y_obs[1:2] + pj[2:3] * y_obs[2:3])
        left1 = res[7:8] - (pj[3:4] * y_obs[0:1] + pj[4:5] * y_obs[1:2] + pj[5:6] * y_obs[2:3])
        terms = x0 * left0 + x1 * left1
        part = nt(jnp.concatenate(split3(terms), axis=0).astype(BF16), cam_hot.astype(BF16))
        rhs = rhs + (part[:8] + part[8:16] + part[16:24])

    rhs_high = rhs.astype(BF16).astype(F32)
    rhs_rows = jnp.concatenate([rhs_high, rhs - rhs_high, jnp.zeros((8, 64), F32)], axis=1)
    product = nt(d_ref[...].reshape(N_CAM * 96, 768), w_ref[...])
    for i in range(2 * N_CAM):
        block = product[i * 48 : (i + 1) * 48]
        tail = block[:, 128:192]
        tail = jnp.concatenate([tail[:24], tail[24:]], axis=1)
        whole = jnp.concatenate([block[:, :128], tail, rhs_rows], axis=0)
        out_ref[i] = whole.astype(BF16)


def last_kernel(got_ref, pairs_ref, schur_ref, rhs_ref):
    total = got_ref[0].astype(F32)
    for i in range(1, got_ref.shape[0]):
        total = total + got_ref[i].astype(F32)
    rhs = total[72:80]
    rhs_ref[...] = rhs[:6, :CAM_DEV] + rhs[:6, CAM_DEV : 2 * CAM_DEV]
    tail = total[48:72]
    tail = jnp.concatenate([tail[:, :64], tail[:, 64:]], axis=0)
    tail = jnp.concatenate([tail, jnp.zeros((48, 64), F32)], axis=1)
    pairs = pairs_ref[...]
    left = (pairs[0:1] & (CAM_DEV - 1))
    right = (pairs[1:2] & (SLICE - 1))
    lefts = jnp.concatenate([left + CAM_DEV * k for k in range(4)], axis=1)
    rights = jnp.concatenate([right] * 6, axis=1)
    pick = jnp.where(
        lax.broadcasted_iota(jnp.int32, (128, 256), 0) == lefts, 1.0, 0.0
    ).astype(BF16)
    first = nn(jnp.concatenate(split3(total[:48]), axis=0).astype(BF16), pick)
    second = nn(jnp.concatenate(split3(tail), axis=0).astype(BF16), pick[:, :128])
    z = jnp.concatenate([first, second], axis=1)
    z = z[:48] + z[48:96] + z[96:]
    keep = lax.broadcasted_iota(jnp.int32, (SLICE, 384), 0) == rights
    rows = [
        jnp.sum(jnp.where(keep, z[l * 8 : (l + 1) * 8], 0.0), axis=0, keepdims=True) for l in range(6)
    ]
    rows = jnp.concatenate(rows, axis=0)
    for k in range(6):
        schur_ref[k * 6 : (k + 1) * 6, :] = rows[:, k * PAIR_DEV : (k + 1) * PAIR_DEV]


def local(cam_jac, pt_jac, resid, obs_cam, obs_pt, pairs, damping):
    vmem = pl.BlockSpec(memory_space=pltpu.VMEM)
    packed = pl.pallas_call(
        pack_kernel,
        out_shape=jax.ShapeDtypeStruct((N_CAM, 16, 768), BF16),
        in_specs=[vmem] * 5,
        out_specs=vmem,
    )(cam_jac, pt_jac, resid, obs_cam.reshape(1, OBS_DEV), obs_pt.reshape(1, OBS_DEV))
    gathered = lax.all_to_all(packed, "cam", 0, 0)
    other = lax.ppermute(gathered, "pts", [(i, i ^ 1) for i in range(N_PTS)])
    send = pl.pallas_call(
        main_kernel,
        out_shape=jax.ShapeDtypeStruct((2 * N_CAM, ROWS, 128), BF16),
        in_specs=[vmem] * 3,
        out_specs=vmem,
        compiler_params=SMALL,
        scratch_shapes=SCRATCH,
    )(damping.reshape(1, 1), gathered, other)
    same = [[2 * i + c for i in range(N_PTS // 2)] for c in range(2)]
    got = lax.all_to_all(send, "pts", 0, 0, axis_index_groups=same)
    return pl.pallas_call(
        last_kernel,
        out_shape=(
            jax.ShapeDtypeStruct((36, PAIR_DEV), F32),
            jax.ShapeDtypeStruct((6, CAM_DEV), F32),
        ),
        in_specs=[vmem, vmem],
        out_specs=(vmem, vmem),
        compiler_params=SMALL,
    )(got, pairs)


def solution(mesh):
    return jax.shard_map(
        local,
        mesh=mesh,
        in_specs=(
            P(None, ("cam", "pts")),
            P(None, ("cam", "pts")),
            P(None, ("cam", "pts")),
            P(("cam", "pts")),
            P(("cam", "pts")),
            P(None, ("cam", "pts")),
            P(),
        ),
        out_specs=(P(None, ("cam", "pts")), P(None, "cam")),
        check_vma=False,
    )
```

time: 46.8 us -> 45.6 us (0.974)
  Pallas kernels: 6.95 us -> 5.7 us
    pallas_call x1, Pallas kernels: 4.56 us -> 3.32 us  [local(): pl.pallas_call(main_kernel, out_shape=jax.ShapeDtypeStruct((2 * N_CAM, RO...]
where the time goes in v3:
time: 45.6 us; the launch traced here: 45.3 us
  blocking collectives  35.9 us (79%)
  Pallas kernels  5.7 us (12%)
  starting transfers between devices  2 us (4%)
  between operations  1.29 us (3%)
    all_to_all x1, blocking collectives, local(): got = lax.all_to_all(send, 'pts', 0, 0, axis_index_groups=same)  23.8 us
    all_to_all x1, blocking collectives, local(): gathered = lax.all_to_all(packed, 'cam', 0, 0)  12.1 us
    pallas_call x1, Pallas kernels, local(): pl.pallas_call(main_kernel, out_shape=jax.ShapeDtypeStruct((2 * N_CAM, RO...  3.32 us
    ppermute x1, starting transfers between devices, local(): other = lax.ppermute(gathered, 'pts', [(i, i ^ 1) for i in range(N_PTS)])  2 us
    pallas_call x1, Pallas kernels, local(): pl.pallas_call(pack_kernel, out_shape=jax.ShapeDtypeStruct((N_CAM, 16, 76...  1.44 us
    pallas_call x1, Pallas kernels, local(): pl.pallas_call(last_kernel, out_shape=(jax.ShapeDtypeStruct((36, PAIR_DEV...  0.94 us
  transfers between devices with their start and end apart: 1, of which 1 were waited for; matrix products, arithmetic and copies ran while one was open for 0% of the time, Pallas kernels for 0%

profile of v3, /device:TPU:1, one launch (start us, length us, event | category | flops | bytes accessed | tf_op | source)
XLA Modules:
  0.0 45.3 jit_solution(15733813444665273319)
XLA Ops:
  0.6 1.4 %shard_map.86 = bf16[8,16,768]{2,1,0:T(8,128)(2,1)} custom-call(bf16[12,512]{1,0:T(8,128)(2,1)} %cj_ref.1, bf16[6,512]{1,0:T(8,128)(2,1)} %pj_ref.1, f32[2,512]{1,0:T(2,128)} %res_ref.1, s32[1,512]{1,0:T(1,128)} %bitcast.4, s32[1,512]{1,0:T(1,128)} %bitcast.5), custom_call_target="tpu_custom_call" | custom-call | tf_op jit(solution)/shard_map/pallas_call | solution.py:200
  2.1 12.1 %all_to_all.10.gat0_ref = bf16[8,16,768]{2,1,0:T(8,128)(2,1)S(1)} all-to-all(bf16[8,16,768]{2,1,0:T(8,128)(2,1)} %shard_map.86), channel_id=1, replica_groups=mesh['cam'=8,'pts'=32] {'cam'}, dimensions={0} | all-to-all | bytes 393216 | tf_op jit(solution)/shard_map/all_to_all | solution.py:206
  14.2 2.0 %collective-permute-start = (bf16[8,16,768]{2,1,0:T(8,128)(2,1)S(1)}, bf16[8,16,768]{2,1,0:T(8,128)(2,1)S(1)}, u32[]{:S(2)}, u32[]{:S(2)}) collective-permute-start(bf16[8,16,768]{2,1,0:T(8,128)(2,1)S(1)} %all_to_all.10.gat0_ref), channel_id=1, source_target_pairs={{0,1},{1,0},{2,3},{3,2},{4,5},{5,4},{6,7},{7,6},{8,9},{9,8},{10,11... | collective-permute-start | bytes 589832 | tf_op jit(solution)/shard_map/ppermute | solution.py:207
  16.8 0.4 collective-permute-done.gat1_ref
  17.3 3.3 %shard_map.87 = bf16[16,80,128]{2,1,0:T(8,128)(2,1)S(1)} custom-call(f32[1,1]{1,0:T(1,128)} %bitcast.3.lam_ref, bf16[8,16,768]{2,1,0:T(8,128)(2,1)S(1)} %all_to_all.10.gat0_ref, bf16[8,16,768]{2,1,0:T(8,128)(2,1)S(1)} %collective-permute-done.gat1_ref), custom_call_target="tpu_custom_call" | custom-call | tf_op jit(solution)/shard_map/pallas_call | solution.py:208
  20.6 0.0 copy-start
  20.6 23.8 %all_to_all.11.got_ref = bf16[16,80,128]{2,1,0:T(8,128)(2,1)S(1)} all-to-all(bf16[16,80,128]{2,1,0:T(8,128)(2,1)S(1)} %shard_map.87), channel_id=1, replica_groups={{0,2,4,6,8,10,12,14,16,18,20,22,24,26,28,30},{1,3,5,7,9,11,13,15,17,19,..., dimensions={0} | all-to-all | bytes 655360 | tf_op jit(solution)/shard_map/all_to_all | solution.py:217
  44.4 0.0 copy-done
  44.4 0.9 %shard_map.88 = (f32[36,64]{1,0:T(8,128)}, f32[6,32]{1,0:T(8,128)}) custom-call(bf16[16,80,128]{2,1,0:T(8,128)(2,1)S(1)} %all_to_all.11.got_ref, s32[2,64]{1,0:T(2,128)S(1)} %copy-done), custom_call_target="tpu_custom_call" | custom-call | tf_op jit(solution)/shard_map/pallas_call | solution.py:218
Async XLA Ops:
  14.2 3.1 %collective-permute-start = (bf16[8,16,768]{2,1,0:T(8,128)(2,1)S(1)}, bf16[8,16,768]{2,1,0:T(8,128)(2,1)S(1)}, u32[]{:S(2)}, u32[]{:S(2)}) collective-permute-start(bf16[8,16,768]{2,1,0:T(8,128)(2,1)S(1)} %all_to_all.10.gat0_ref), channel_id=1, source_target_pairs={{0,1},{1,0},{2,3},{3,2},{4,5},{5,4},{6,7},{7,6},{8,9},{9,8},{10,11... | collective-permute-start | bytes 589832 | tf_op jit(solution)/shard_map/ppermute | solution.py:207
  20.6 23.8 %copy-start = (s32[2,64]{1,0:T(2,128)S(1)}, s32[2,64]{1,0:T(2,128)}, u32[]{:S(2)}) copy-start(s32[2,64]{1,0:T(2,128)} %pairs_ref.1) | copy-start | bytes 1540

commit v4 on v3

--- a/solution.py
+++ b/solution.py
@@ -15,9 +15,9 @@
 ROWS = 80
 F32 = jnp.float32
 BF16 = jnp.bfloat16
-UNROLL = 4
+UNROLL = 8
 SMALL = pltpu.CompilerParams(vmem_limit_bytes=16 * 1024 * 1024)
-SCRATCH = [pltpu.VMEM((N_CAM, 96, 768), BF16), pltpu.VMEM((192, 768), BF16)]
+SCRATCH = [pltpu.VMEM((N_CAM, 96, 384), BF16), pltpu.VMEM((2, 192, 384), BF16)]
 
 
 def split3(x):
@@ -53,9 +53,9 @@
 
 
 def unpack(m):
-    x = m[:, :OBS_DEV].astype(F32)
-    y = m[:, OBS_DEV:].astype(F32)
-    return x[:8], x[8:], jnp.concatenate([y[:8], y[8:]], axis=1)
+    x = m.astype(F32)
+    x1 = jnp.concatenate([x[6:12], x[12:14] + x[14:16]], axis=0)
+    return x[:8], x1, x[16:24]
 
 
 def spread(x0, x1, pj, hots):
@@ -69,10 +69,9 @@
 
 
 def stat_rows(x0, x1, pj):
-    res = x0 + x1
     jp = [pj[i : i + 1] for i in range(6)]
-    r0 = res[6:7]
-    r1 = res[7:8]
+    r0 = x1[6:7]
+    r1 = x1[7:8]
     rows = [jp[s] * jp[t] + jp[3 + s] * jp[3 + t] for s, t in
             ((0, 0), (0, 1), (0, 2), (1, 1), (1, 2), (2, 2))]
     rows = rows + [jp[s] * r0 + jp[3 + s] * r1 for s in range(3)]
@@ -100,33 +99,42 @@
     return full, y
 
 
-def main_kernel(lam_ref, gat0_ref, gat1_ref, out_ref, d_ref, w_ref):
+def cells(pj, iotac):
+    half = jnp.where(pj[6:7] >= 16.0, 1.0, 0.0)
+    cell_hot = jnp.where(iotac == pj[7:8] + half * PT_DEV, 1.0, 0.0).astype(BF16)
+    return pj[6:7] - half * 16.0, cell_hot
+
+
+def build_range(gat_ref, d_ref):
+    core = lax.axis_index("pts") % 2
+    first = (lax.broadcasted_iota(jnp.int32, (SLICE, OBS_DEV), 0) + core * SLICE).astype(F32)
+    iotac = lax.broadcasted_iota(jnp.int32, (2 * PT_DEV, OBS_DEV), 0).astype(F32)
+
+    def one_group(g, totals):
+        x0, x1, pj = unpack(gat_ref[g])
+        low, cell_hot = cells(pj, iotac)
+        hot = jnp.where(first == low, 1.0, 0.0)
+        left = spread(x0, x1, pj, [hot]) + stat_rows(x0, x1, pj)
+        grid = nt(jnp.concatenate(left, axis=0).astype(BF16), cell_hot)
+        for s in range(3):
+            part = grid[s * 48 : (s + 1) * 48].astype(BF16)
+            d_ref[g, :48, s * PT_DEV : (s + 1) * PT_DEV] = part[:, :PT_DEV]
+            d_ref[g, 48:, s * PT_DEV : (s + 1) * PT_DEV] = part[:, PT_DEV:]
+        return totals + (grid[144:176, :PT_DEV] + grid[144:176, PT_DEV:])
+
+    return lax.fori_loop(0, N_CAM, one_group, jnp.zeros((32, PT_DEV), F32), unroll=UNROLL)
+
+
+def first_kernel(gat_ref, d_ref, totals_ref):
+    totals_ref[...] = build_range(gat_ref, d_ref)
+
+
+def main_kernel(lam_ref, totals_ref, d0_ref, gat0_ref, gat1_ref, out_ref, d1_ref, w_ref):
     group = lax.axis_index("cam")
-    core = lax.axis_index("pts") % 2
     gat_refs = (gat0_ref, gat1_ref)
-    iota8 = lax.broadcasted_iota(jnp.int32, (SLICE, OBS_DEV), 0) + core * SLICE
-    firsts = [(iota8 + h * 2 * SLICE).astype(F32) for h in range(2)]
-    iota32 = lax.broadcasted_iota(jnp.int32, (CAM_DEV, OBS_DEV), 0).astype(F32)
-    iotap = lax.broadcasted_iota(jnp.int32, (PT_DEV, OBS_DEV), 0).astype(F32)
-
-    def one_group(g, totals):
-        after = []
-        for r in range(2):
-            x0, x1, pj = unpack(gat_refs[r][g])
-            hots = [jnp.where(f == pj[6:7], 1.0, 0.0) for f in firsts]
-            left = spread(x0, x1, pj, hots) + stat_rows(x0, x1, pj)
-            left = jnp.concatenate(left, axis=0).astype(BF16)
-            pt_hot = jnp.where(iotap == pj[7:8], 1.0, 0.0).astype(BF16)
-            grid = nt(left, pt_hot)
-            for s in range(3):
-                at = (r * 3 + s) * PT_DEV
-                d_ref[g, :, at : at + PT_DEV] = grid[s * 96 : (s + 1) * 96].astype(BF16)
-            after.append(totals[r] + grid[288:320])
-        return tuple(after)
-
-    zero = jnp.zeros((32, PT_DEV), F32)
-    totals = lax.fori_loop(0, N_CAM, one_group, (zero, zero), unroll=UNROLL)
-    totals = jnp.concatenate(totals, axis=1)
+    iota16 = lax.broadcasted_iota(jnp.int32, (16, OBS_DEV), 0).astype(F32)
+    iotac = lax.broadcasted_iota(jnp.int32, (2 * PT_DEV, OBS_DEV), 0).astype(F32)
+    totals = jnp.concatenate([totals_ref[...], build_range(gat1_ref, d1_ref)], axis=1)
     eight = totals[:8] + totals[8:16] + totals[16:24]
     ninth = totals[24:25] + totals[25:26] + totals[26:27]
     full, y = point_inverse([eight[i : i + 1] for i in range(8)] + [ninth], lam_ref[...])
@@ -135,28 +143,33 @@
     for r in range(2):
         mine = slice(r * PT_DEV, (r + 1) * PT_DEV)
         x0, x1, pj = unpack(gat_refs[r][group])
-        cam_hot = jnp.where(iota32 == pj[6:7], 1.0, 0.0)
-        pt_hot = jnp.where(iotap == pj[7:8], 1.0, 0.0).astype(BF16)
-        left = jnp.concatenate(spread(x0, x1, pj, [cam_hot]), axis=0).astype(BF16)
-        grid = nt(left, pt_hot)
+        low, cell_hot = cells(pj, iotac)
+        hot = jnp.where(iota16 == low, 1.0, 0.0)
+        left = jnp.concatenate(spread(x0, x1, pj, [hot]), axis=0).astype(BF16)
+        grid = nt(left, cell_hot)
         for t in range(3):
-            value = (grid[:192] * full[0][t][:, mine] + grid[192:384] * full[1][t][:, mine]
-                     + grid[384:] * full[2][t][:, mine])
-            at = (r * 3 + t) * PT_DEV
-            w_ref[:, at : at + PT_DEV] = value.astype(BF16)
+            scale = [jnp.concatenate([full[s][t][:, mine]] * 2, axis=1) for s in range(3)]
+            value = (grid[:96] * scale[0] + grid[96:192] * scale[1] + grid[192:] * scale[2]).astype(BF16)
+            at = t * PT_DEV
+            for k in range(6):
+                for h in range(2):
+                    w_ref[r, k * 32 + h * 16 : k * 32 + (h + 1) * 16, at : at + PT_DEV] = (
+                        value[k * 16 : (k + 1) * 16, h * PT_DEV : (h + 1) * PT_DEV])
         y8 = jnp.concatenate([v[:, mine] for v in y] + [jnp.zeros((5, PT_DEV), F32)], axis=0)
-        y_obs = nn(jnp.concatenate(split3(y8), axis=0).astype(BF16), pt_hot)
+        y8 = jnp.concatenate([y8, y8], axis=1)
+        y_obs = nn(jnp.concatenate(split3(y8), axis=0).astype(BF16), cell_hot)
         y_obs = y_obs[:8] + y_obs[8:16] + y_obs[16:24]
-        res = x0 + x1
-        left0 = res[6:7] - (pj[0:1] * y_obs[0:1] + pj[1:2] * y_obs[1:2] + pj[2:3] * y_obs[2:3])
-        left1 = res[7:8] - (pj[3:4] * y_obs[0:1] + pj[4:5] * y_obs[1:2] + pj[5:6] * y_obs[2:3])
+        left0 = x1[6:7] - (pj[0:1] * y_obs[0:1] + pj[1:2] * y_obs[1:2] + pj[2:3] * y_obs[2:3])
+        left1 = x1[7:8] - (pj[3:4] * y_obs[0:1] + pj[4:5] * y_obs[1:2] + pj[5:6] * y_obs[2:3])
         terms = x0 * left0 + x1 * left1
-        part = nt(jnp.concatenate(split3(terms), axis=0).astype(BF16), cam_hot.astype(BF16))
+        cam_hot = jnp.where(iotac[:CAM_DEV] == pj[6:7], 1.0, 0.0).astype(BF16)
+        part = nt(jnp.concatenate(split3(terms), axis=0).astype(BF16), cam_hot)
         rhs = rhs + (part[:8] + part[8:16] + part[16:24])
 
     rhs_high = rhs.astype(BF16).astype(F32)
     rhs_rows = jnp.concatenate([rhs_high, rhs - rhs_high, jnp.zeros((8, 64), F32)], axis=1)
-    product = nt(d_ref[...].reshape(N_CAM * 96, 768), w_ref[...])
+    product = nt(d0_ref[...].reshape(N_CAM * 96, 384), w_ref[0])
+    product = product + nt(d1_ref[...].reshape(N_CAM * 96, 384), w_ref[1])
     for i in range(2 * N_CAM):
         block = product[i * 48 : (i + 1) * 48]
         tail = block[:, 128:192]
@@ -197,22 +210,43 @@
 
 def local(cam_jac, pt_jac, resid, obs_cam, obs_pt, pairs, damping):
     vmem = pl.BlockSpec(memory_space=pltpu.VMEM)
-    packed = pl.pallas_call(
-        pack_kernel,
-        out_shape=jax.ShapeDtypeStruct((N_CAM, 16, 768), BF16),
-        in_specs=[vmem] * 5,
-        out_specs=vmem,
-    )(cam_jac, pt_jac, resid, obs_cam.reshape(1, OBS_DEV), obs_pt.reshape(1, OBS_DEV))
+    def rows(x, at):
+        return jnp.pad(x, ((at, 24 - at - x.shape[0]), (0, 0)))
+
+    cell = lax.broadcasted_iota(jnp.int32, (24, OBS_DEV), 0) * OBS_DEV
+    cell = cell + lax.broadcasted_iota(jnp.int32, (24, OBS_DEV), 1)
+
+    def code(x, mask, at):
+        keep = jnp.where((cell >= at * OBS_DEV) & (cell < (at + 1) * OBS_DEV), mask, 0)
+        return lax.broadcast_in_dim(x, (24, OBS_DEV), (1,)) & keep
+
+    cam = code(obs_cam, CAM_DEV - 1, 22)
+    pt = code(obs_pt, PT_DEV - 1, 23)
+    second = rows(resid, 14)
+    packed = ((rows(cam_jac, 0) + rows(pt_jac, 16)).astype(F32) + (cam + pt).astype(F32) + rows(resid, 12)
+              + (second - lax.reduce_precision(second, 8, 7))).astype(BF16)
+    packed = jnp.broadcast_to(packed[None], (N_CAM, 24, OBS_DEV))
     gathered = lax.all_to_all(packed, "cam", 0, 0)
     other = lax.ppermute(gathered, "pts", [(i, i ^ 1) for i in range(N_PTS)])
+    d0, totals = pl.pallas_call(
+        first_kernel,
+        out_shape=(
+            jax.ShapeDtypeStruct((N_CAM, 96, 384), BF16),
+            jax.ShapeDtypeStruct((32, PT_DEV), F32),
+        ),
+        in_specs=[vmem],
+        out_specs=(vmem, vmem),
+        compiler_params=SMALL,
+        cost_estimate=pl.CostEstimate(flops=10**9, bytes_accessed=10**6, transcendentals=0),
+    )(gathered)
     send = pl.pallas_call(
         main_kernel,
         out_shape=jax.ShapeDtypeStruct((2 * N_CAM, ROWS, 128), BF16),
-        in_specs=[vmem] * 3,
+        in_specs=[vmem] * 5,
         out_specs=vmem,
         compiler_params=SMALL,
         scratch_shapes=SCRATCH,
-    )(damping.reshape(1, 1), gathered, other)
+    )(damping.reshape(1, 1), totals, d0, gathered, other)
     same = [[2 * i + c for i in range(N_PTS // 2)] for c in range(2)]
     got = lax.all_to_all(send, "pts", 0, 0, axis_index_groups=same)
     return pl.pallas_call(

time: 45.6 us -> 44.3 us (0.971)
  Pallas kernels: 5.7 us -> 4.12 us
  other arithmetic: 0 us -> 0.91 us
    pallas_call x1, Pallas kernels: 3.32 us -> 2.16 us  [local(): pl.pallas_call(main_kernel, out_shape=jax.ShapeDtypeStruct((2 * N_CAM, RO...]
    convert_element_type x0 -> x1, other arithmetic: none -> 0.9 us  [local(): packed = ((rows(cam_jac, 0) + rows(pt_jac, 16)).astype(F32) + (cam + pt)....]
  transfers between devices with their start and end apart: 1 -> 1, of which waited for: 1 -> 0; matrix products, arithmetic and copies ran while one was open for 0% -> 0% of each run, Pallas kernels for 0% -> 2%
where the time goes in v4:
time: 44.3 us; the launch traced here: 44.1 us
  blocking collectives  35.7 us (81%)
  Pallas kernels  4.12 us (9%)
  starting transfers between devices  2 us (5%)
  between operations  1.32 us (3%)
  other arithmetic  0.91 us (2%)
    all_to_all x1, blocking collectives, local(): got = lax.all_to_all(send, 'pts', 0, 0, axis_index_groups=same)  23.8 us
    all_to_all x1, blocking collectives, local(): gathered = lax.all_to_all(packed, 'cam', 0, 0)  11.9 us
    pallas_call x1, Pallas kernels, local(): pl.pallas_call(main_kernel, out_shape=jax.ShapeDtypeStruct((2 * N_CAM, RO...  2.16 us
    ppermute x1, starting transfers between devices, local(): other = lax.ppermute(gathered, 'pts', [(i, i ^ 1) for i in range(N_PTS)])  2 us
    pallas_call x1, Pallas kernels, local(): pl.pallas_call(first_kernel, out_shape=(jax.ShapeDtypeStruct((N_CAM, 96,...  1.02 us
    pallas_call x1, Pallas kernels, local(): pl.pallas_call(last_kernel, out_shape=(jax.ShapeDtypeStruct((36, PAIR_DEV...  0.94 us
    convert_element_type x1, other arithmetic, local(): packed = ((rows(cam_jac, 0) + rows(pt_jac, 16)).astype(F32) + (cam + pt)....  0.9 us
  transfers between devices with their start and end apart: 1, of which 0 were waited for; matrix products, arithmetic and copies ran while one was open for 0% of the time, Pallas kernels for 2%

profile of v4, /device:TPU:1, one launch (start us, length us, event | category | flops | bytes accessed | tf_op | source)
XLA Modules:
  0.0 44.1 jit_solution(18122573254523707630)
XLA Ops:
  0.6 0.9 %fusion.1 = bf16[24,512]{1,0:T(8,128)(2,1)S(1)} fusion(f32[2,512]{1,0:T(2,128)} %param.9, s32[512]{0:T(512)} %param.11, s32[24]{0:T(128)S(1)} %iota_multiply_fusion, s32[512]{0:T(512)} %param.10, bf16[6,512]{1,0:T(8,128)(2,1)} %param.8, bf16[12,512]{1,0:T(8,128)(2,1)} %param.7), kind=kLoop, calls=%fused_computation.2 | loop fusion | flops 282624 | bytes 51296 | tf_op jit(solution)/shard_map/convert_element_type | solution.py:227
  1.6 11.9 %all_to_all.10.gat_ref.gat0_ref = bf16[8,24,512]{2,1,0:T(8,128)(2,1)S(1)} all-to-all(bf16[8,24,512]{2,1,0:T(8,128)(2,1)S(1)} %broadcast_in_dim.29), channel_id=1, replica_groups=mesh['cam'=8,'pts'=32] {'cam'}, dimensions={0} | all-to-all | bytes 393216 | tf_op jit(solution)/shard_map/all_to_all | solution.py:229
  13.5 2.0 %collective-permute-start = (bf16[8,24,512]{2,1,0:T(8,128)(2,1)S(1)}, bf16[8,24,512]{2,1,0:T(8,128)(2,1)S(1)}, u32[]{:S(2)}, u32[]{:S(2)}) collective-permute-start(bf16[8,24,512]{2,1,0:T(8,128)(2,1)S(1)} %all_to_all.10.gat_ref.gat0_ref), channel_id=1, source_target_pairs={{0,1},{1,0},{2,3},{3,2},{4,5},{5,4},{6,7},{7,6},{8,9},{9,8},{10,11... | collective-permute-start | bytes 589832 | tf_op jit(solution)/shard_map/ppermute | solution.py:230
  16.1 1.0 %shard_map.86 = (bf16[8,96,384]{2,1,0:T(8,128)(2,1)S(1)}, f32[32,128]{1,0:T(8,128)S(1)}) custom-call(bf16[8,24,512]{2,1,0:T(8,128)(2,1)S(1)} %all_to_all.10.gat_ref.gat0_ref), custom_call_target="tpu_custom_call" | custom-call | flops 1000000000 | bytes 1000000 | tf_op jit(solution)/shard_map/pallas_call | solution.py:231
  17.2 0.0 collective-permute-done.gat1_ref
  17.2 2.2 %shard_map.87 = bf16[16,80,128]{2,1,0:T(8,128)(2,1)S(1)} custom-call(f32[1,1]{1,0:T(1,128)} %bitcast.1.lam_ref, f32[32,128]{1,0:T(8,128)S(1)} %get-tuple-element.4.totals_ref, bf16[8,96,384]{2,1,0:T(8,128)(2,1)S(1)} %get-tuple-element.5.d0_ref, bf16[8,24,512]{2,1,0:T(8,128)(2,1)S(1)} %all_to_all.10.gat_ref.gat0_ref, ...), custom_call_target="tpu_custom_call" | custom-call | tf_op jit(solution)/shard_map/pallas_call | solution.py:242
  19.3 0.0 copy-start
  19.3 23.8 %all_to_all.11.got_ref = bf16[16,80,128]{2,1,0:T(8,128)(2,1)S(1)} all-to-all(bf16[16,80,128]{2,1,0:T(8,128)(2,1)S(1)} %shard_map.87), channel_id=1, replica_groups={{0,2,4,6,8,10,12,14,16,18,20,22,24,26,28,30},{1,3,5,7,9,11,13,15,17,19,..., dimensions={0} | all-to-all | bytes 655360 | tf_op jit(solution)/shard_map/all_to_all | solution.py:251
  43.1 0.0 copy-done
  43.1 0.9 %shard_map.88 = (f32[36,64]{1,0:T(8,128)}, f32[6,32]{1,0:T(8,128)}) custom-call(bf16[16,80,128]{2,1,0:T(8,128)(2,1)S(1)} %all_to_all.11.got_ref, s32[2,64]{1,0:T(2,128)S(1)} %copy-done), custom_call_target="tpu_custom_call" | custom-call | tf_op jit(solution)/shard_map/pallas_call | solution.py:252
  (2 shorter events, 0.0 us)
Async XLA Ops:
  13.5 3.7 %collective-permute-start = (bf16[8,24,512]{2,1,0:T(8,128)(2,1)S(1)}, bf16[8,24,512]{2,1,0:T(8,128)(2,1)S(1)}, u32[]{:S(2)}, u32[]{:S(2)}) collective-permute-start(bf16[8,24,512]{2,1,0:T(8,128)(2,1)S(1)} %all_to_all.10.gat_ref.gat0_ref), channel_id=1, source_target_pairs={{0,1},{1,0},{2,3},{3,2},{4,5},{5,4},{6,7},{7,6},{8,9},{9,8},{10,11... | collective-permute-start | bytes 589832 | tf_op jit(solution)/shard_map/ppermute | solution.py:230
  19.3 23.8 %copy-start = (s32[2,64]{1,0:T(2,128)S(1)}, s32[2,64]{1,0:T(2,128)}, u32[]{:S(2)}) copy-start(s32[2,64]{1,0:T(2,128)} %pairs_ref.1) | copy-start | bytes 1540

commit v5 on v4

--- a/solution.py
+++ b/solution.py
@@ -125,8 +125,15 @@
     return lax.fori_loop(0, N_CAM, one_group, jnp.zeros((32, PT_DEV), F32), unroll=UNROLL)
 
 
-def first_kernel(gat_ref, d_ref, totals_ref):
+def first_kernel(gat_ref, pairs_ref, d_ref, totals_ref, near_ref):
+    near_ref[...] = pairs_ref[...]
     totals_ref[...] = build_range(gat_ref, d_ref)
+
+
+def fit(x):
+    most = jnp.max(jnp.max(jnp.abs(x), axis=0, keepdims=True), axis=1, keepdims=True)
+    power = jnp.floor(jnp.log2(jnp.maximum(most, 1e-30)))
+    return power, jnp.exp2(14.0 - power)
 
 
 def main_kernel(lam_ref, totals_ref, d0_ref, gat0_ref, gat1_ref, out_ref, d1_ref, w_ref):
@@ -166,24 +173,32 @@
         part = nt(jnp.concatenate(split3(terms), axis=0).astype(BF16), cam_hot)
         rhs = rhs + (part[:8] + part[8:16] + part[16:24])
 
-    rhs_high = rhs.astype(BF16).astype(F32)
-    rhs_rows = jnp.concatenate([rhs_high, rhs - rhs_high, jnp.zeros((8, 64), F32)], axis=1)
     product = nt(d0_ref[...].reshape(N_CAM * 96, 384), w_ref[0])
     product = product + nt(d1_ref[...].reshape(N_CAM * 96, 384), w_ref[1])
+    power, scale = fit(product)
+    rhs_power, rhs_scale = fit(rhs)
+    rhs = rhs * rhs_scale
+    rhs_high = rhs.astype(BF16).astype(F32)
+    rhs_rows = jnp.concatenate(
+        [rhs_high, rhs - rhs_high, jnp.broadcast_to(power, (8, 32)), jnp.broadcast_to(rhs_power, (8, 32))],
+        axis=1,
+    )
     for i in range(2 * N_CAM):
-        block = product[i * 48 : (i + 1) * 48]
+        block = product[i * 48 : (i + 1) * 48] * scale
         tail = block[:, 128:192]
         tail = jnp.concatenate([tail[:24], tail[24:]], axis=1)
-        whole = jnp.concatenate([block[:, :128], tail, rhs_rows], axis=0)
-        out_ref[i] = whole.astype(BF16)
+        out_ref[i] = jnp.concatenate([block[:, :128], tail, rhs_rows], axis=0)
 
 
 def last_kernel(got_ref, pairs_ref, schur_ref, rhs_ref):
-    total = got_ref[0].astype(F32)
-    for i in range(1, got_ref.shape[0]):
-        total = total + got_ref[i].astype(F32)
-    rhs = total[72:80]
-    rhs_ref[...] = rhs[:6, :CAM_DEV] + rhs[:6, CAM_DEV : 2 * CAM_DEV]
+    total = jnp.zeros((72, 128), F32)
+    rhs = jnp.zeros((8, CAM_DEV), F32)
+    for i in range(got_ref.shape[0]):
+        part = got_ref[i].astype(F32)
+        scales = jnp.exp2(part[72:73] - 14.0)
+        total = total + part[:72] * scales[:, 64:65]
+        rhs = rhs + (part[72:80, :32] + part[72:80, 32:64]) * scales[:, 96:97]
+    rhs_ref[...] = rhs[:6]
     tail = total[48:72]
     tail = jnp.concatenate([tail[:, :64], tail[:, 64:]], axis=0)
     tail = jnp.concatenate([tail, jnp.zeros((48, 64), F32)], axis=1)
@@ -228,27 +243,28 @@
     packed = jnp.broadcast_to(packed[None], (N_CAM, 24, OBS_DEV))
     gathered = lax.all_to_all(packed, "cam", 0, 0)
     other = lax.ppermute(gathered, "pts", [(i, i ^ 1) for i in range(N_PTS)])
-    d0, totals = pl.pallas_call(
+    d0, totals, near = pl.pallas_call(
         first_kernel,
         out_shape=(
             jax.ShapeDtypeStruct((N_CAM, 96, 384), BF16),
             jax.ShapeDtypeStruct((32, PT_DEV), F32),
+            jax.ShapeDtypeStruct((2, PAIR_DEV), jnp.int32),
         ),
-        in_specs=[vmem],
-        out_specs=(vmem, vmem),
+        in_specs=[vmem] * 2,
+        out_specs=(vmem,) * 3,
         compiler_params=SMALL,
         cost_estimate=pl.CostEstimate(flops=10**9, bytes_accessed=10**6, transcendentals=0),
-    )(gathered)
+    )(gathered, pairs)
     send = pl.pallas_call(
         main_kernel,
-        out_shape=jax.ShapeDtypeStruct((2 * N_CAM, ROWS, 128), BF16),
+        out_shape=jax.ShapeDtypeStruct((2 * N_CAM, ROWS, 128), F32),
         in_specs=[vmem] * 5,
         out_specs=vmem,
         compiler_params=SMALL,
         scratch_shapes=SCRATCH,
     )(damping.reshape(1, 1), totals, d0, gathered, other)
     same = [[2 * i + c for i in range(N_PTS // 2)] for c in range(2)]
-    got = lax.all_to_all(send, "pts", 0, 0, axis_index_groups=same)
+    got = lax.all_to_all(send.astype(jnp.float16), "pts", 0, 0, axis_index_groups=same).astype(F32)
     return pl.pallas_call(
         last_kernel,
         out_shape=(
@@ -258,7 +274,7 @@
         in_specs=[vmem, vmem],
         out_specs=(vmem, vmem),
         compiler_params=SMALL,
-    )(got, pairs)
+    )(got, near)
 
 
 def solution(mesh):

time: 44.3 us -> 44.7 us (level)
  no operation moved by 1% of the time
where the time goes in v5:
time: 44.7 us; the launch traced here: 44.5 us
  blocking collectives  35.7 us (80%)
  Pallas kernels  4.41 us (10%)
  starting transfers between devices  2 us (4%)
  between operations  1.34 us (3%)
  other arithmetic  1 us (2%)
    all_to_all x1, blocking collectives, local(): lax.all_to_all(send.astype(jnp.float16), 'pts', 0, 0, axis_index_groups=s...  23.8 us
    all_to_all x1, blocking collectives, local(): gathered = lax.all_to_all(packed, 'cam', 0, 0)  11.9 us
    pallas_call x1, Pallas kernels, local(): pl.pallas_call(main_kernel, out_shape=jax.ShapeDtypeStruct((2 * N_CAM, RO...  2.33 us
    ppermute x1, starting transfers between devices, local(): other = lax.ppermute(gathered, 'pts', [(i, i ^ 1) for i in range(N_PTS)])  2 us
    pallas_call x1, Pallas kernels, local(): pl.pallas_call(last_kernel, out_shape=(jax.ShapeDtypeStruct((36, PAIR_DEV...  1.05 us
    pallas_call x1, Pallas kernels, local(): pl.pallas_call(first_kernel, out_shape=(jax.ShapeDtypeStruct((N_CAM, 96,...  1.02 us
    convert_element_type x1, other arithmetic, local(): packed = ((rows(cam_jac, 0) + rows(pt_jac, 16)).astype(F32) + (cam + pt)....  0.9 us
  transfers between devices with their start and end apart: 1, of which 0 were waited for; matrix products, arithmetic and copies ran while one was open for 0% of the time, Pallas kernels for 2%

profile of v5, /device:TPU:1, one launch (start us, length us, event | category | flops | bytes accessed | tf_op | source)
XLA Modules:
  0.0 44.5 jit_solution(16277567689635341106)
XLA Ops:
  0.6 0.9 %fusion.1 = bf16[24,512]{1,0:T(8,128)(2,1)S(1)} fusion(f32[2,512]{1,0:T(2,128)} %param.9, s32[512]{0:T(512)} %param.11, s32[24]{0:T(128)S(1)} %iota_multiply_fusion, s32[512]{0:T(512)} %param.10, bf16[6,512]{1,0:T(8,128)(2,1)} %param.8, bf16[12,512]{1,0:T(8,128)(2,1)} %param.7), kind=kLoop, calls=%fused_computation.2 | loop fusion | flops 282624 | bytes 51296 | tf_op jit(solution)/shard_map/convert_element_type | solution.py:242
  1.6 11.9 %all_to_all.10.gat_ref.gat0_ref = bf16[8,24,512]{2,1,0:T(8,128)(2,1)S(1)} all-to-all(bf16[8,24,512]{2,1,0:T(8,128)(2,1)S(1)} %broadcast_in_dim.29), channel_id=1, replica_groups=mesh['cam'=8,'pts'=32] {'cam'}, dimensions={0} | all-to-all | bytes 393216 | tf_op jit(solution)/shard_map/all_to_all | solution.py:244
  13.5 0.0 copy-start
  13.5 2.0 %collective-permute-start = (bf16[8,24,512]{2,1,0:T(8,128)(2,1)S(1)}, bf16[8,24,512]{2,1,0:T(8,128)(2,1)S(1)}, u32[]{:S(2)}, u32[]{:S(2)}) collective-permute-start(bf16[8,24,512]{2,1,0:T(8,128)(2,1)S(1)} %all_to_all.10.gat_ref.gat0_ref), channel_id=1, source_target_pairs={{0,1},{1,0},{2,3},{3,2},{4,5},{5,4},{6,7},{7,6},{8,9},{9,8},{10,11... | collective-permute-start | bytes 589832 | tf_op jit(solution)/shard_map/ppermute | solution.py:245
  16.1 0.0 copy-done
  16.1 1.0 %shard_map.86 = (bf16[8,96,384]{2,1,0:T(8,128)(2,1)S(1)}, f32[32,128]{1,0:T(8,128)S(1)}, s32[2,64]{1,0:T(2,128)S(1)}) custom-call(bf16[8,24,512]{2,1,0:T(8,128)(2,1)S(1)} %all_to_all.10.gat_ref.gat0_ref, s32[2,64]{1,0:T(2,128)S(1)} %copy-done), custom_call_target="tpu_custom_call" | custom-call | flops 1000000000 | bytes 1000000 | tf_op jit(solution)/shard_map/pallas_call | solution.py:246
  17.2 0.0 collective-permute-done.gat1_ref
  17.2 2.3 %shard_map.87 = f32[16,80,128]{2,1,0:T(8,128)S(1)} custom-call(f32[1,1]{1,0:T(1,128)} %bitcast.1.lam_ref, f32[32,128]{1,0:T(8,128)S(1)} %get-tuple-element.5.totals_ref, bf16[8,96,384]{2,1,0:T(8,128)(2,1)S(1)} %get-tuple-element.6.d0_ref, bf16[8,24,512]{2,1,0:T(8,128)(2,1)S(1)} %all_to_all.10.gat_ref.gat0_ref, ...), custom_call_target="tpu_custom_call" | custom-call | tf_op jit(solution)/shard_map/pallas_call | solution.py:258
  19.6 23.8 %all_to_all.11 = f16[16,80,128]{2,1,0:T(8,128)(2,1)S(1)} all-to-all(f16[16,80,128]{2,1,0:T(8,128)(2,1)S(1)} %convert_element_type.26), channel_id=1, replica_groups={{0,2,4,6,8,10,12,14,16,18,20,22,24,26,28,30},{1,3,5,7,9,11,13,15,17,19,..., dimensions={0} | all-to-all | bytes 655360 | tf_op jit(solution)/shard_map/all_to_all | solution.py:267
  43.4 1.1 %shard_map.88 = (f32[36,64]{1,0:T(8,128)}, f32[6,32]{1,0:T(8,128)}) custom-call(f32[16,80,128]{2,1,0:T(8,128)S(1)} %convert_element_type.27.got_ref, s32[2,64]{1,0:T(2,128)S(1)} %get-tuple-element.7.pairs_ref), custom_call_target="tpu_custom_call" | custom-call | tf_op jit(solution)/shard_map/pallas_call | solution.py:268
  (4 shorter events, 0.1 us)
Async XLA Ops:
  13.5 2.7 %copy-start = (s32[2,64]{1,0:T(2,128)S(1)}, s32[2,64]{1,0:T(2,128)}, u32[]{:S(2)}) copy-start(s32[2,64]{1,0:T(2,128)} %pairs_ref.1) | copy-start | bytes 1540
  13.5 3.7 %collective-permute-start = (bf16[8,24,512]{2,1,0:T(8,128)(2,1)S(1)}, bf16[8,24,512]{2,1,0:T(8,128)(2,1)S(1)}, u32[]{:S(2)}, u32[]{:S(2)}) collective-permute-start(bf16[8,24,512]{2,1,0:T(8,128)(2,1)S(1)} %all_to_all.10.gat_ref.gat0_ref), channel_id=1, source_target_pairs={{0,1},{1,0},{2,3},{3,2},{4,5},{5,4},{6,7},{7,6},{8,9},{9,8},{10,11... | collective-permute-start | bytes 589832 | tf_op jit(solution)/shard_map/ppermute | solution.py:245

commit v6 on v5

--- a/solution.py
+++ b/solution.py
@@ -16,6 +16,7 @@
 F32 = jnp.float32
 BF16 = jnp.bfloat16
 UNROLL = 8
+ORDERS = ([4 * (y if z % 2 == 0 else 3 - y) + z for z in range(4) for y in range(4)], [4 * (y if z % 2 == 0 else 3 - y) + z for z in range(4) for y in range(4)][::-1], [4 * (y if z % 2 == 0 else 3 - y) + z for z in range(4) for y in range(4)][::-1], [4 * (y if z % 2 == 0 else 3 - y) + z for z in range(4) for y in range(4)])
 SMALL = pltpu.CompilerParams(vmem_limit_bytes=16 * 1024 * 1024)
 SCRATCH = [pltpu.VMEM((N_CAM, 96, 384), BF16), pltpu.VMEM((2, 192, 384), BF16)]
 
@@ -138,6 +139,7 @@
 
 def main_kernel(lam_ref, totals_ref, d0_ref, gat0_ref, gat1_ref, out_ref, d1_ref, w_ref):
     group = lax.axis_index("cam")
+    turn = (group % 2) * 2 + lax.axis_index("pts") % 2
     gat_refs = (gat0_ref, gat1_ref)
     iota16 = lax.broadcasted_iota(jnp.int32, (16, OBS_DEV), 0).astype(F32)
     iotac = lax.broadcasted_iota(jnp.int32, (2 * PT_DEV, OBS_DEV), 0).astype(F32)
@@ -187,7 +189,9 @@
         block = product[i * 48 : (i + 1) * 48] * scale
         tail = block[:, 128:192]
         tail = jnp.concatenate([tail[:24], tail[24:]], axis=1)
-        out_ref[i] = jnp.concatenate([block[:, :128], tail, rhs_rows], axis=0)
+        places = [order.index(i) for order in ORDERS]
+        at = jnp.where(turn < 2, jnp.where(turn == 0, places[0], places[1]), jnp.where(turn == 2, places[2], places[3]))
+        out_ref[at] = jnp.concatenate([block[:, :128], tail, rhs_rows], axis=0)
 
 
 def last_kernel(got_ref, pairs_ref, schur_ref, rhs_ref):
@@ -263,8 +267,8 @@
         compiler_params=SMALL,
         scratch_shapes=SCRATCH,
     )(damping.reshape(1, 1), totals, d0, gathered, other)
-    same = [[2 * i + c for i in range(N_PTS // 2)] for c in range(2)]
-    got = lax.all_to_all(send.astype(jnp.float16), "pts", 0, 0, axis_index_groups=same).astype(F32)
+    same = [[g * N_PTS + 2 * i + c for i in ORDERS[g % 2 * 2 + c]] for g in range(N_CAM) for c in range(2)]
+    got = lax.all_to_all(send.astype(jnp.float16), ("cam", "pts"), 0, 0, axis_index_groups=same).astype(F32)
     return pl.pallas_call(
         last_kernel,
         out_shape=(

time: 44.7 us -> 40.7 us (0.911)
  the two profiles are of different devices: /device:TPU:1 before, /device:TPU:64 now
where the time goes in v6:
time: 40.7 us; the launch traced here: 40.5 us
  blocking collectives  33.7 us (83%)
  Pallas kernels  4.41 us (11%)
  between operations  1.34 us (3%)
  other arithmetic  1 us (2%)
    all_to_all x1, blocking collectives, local(): lax.all_to_all(send.astype(jnp.float16), ('cam', 'pts'), 0, 0, axis_index...  21.3 us
    all_to_all x1, blocking collectives, local(): gathered = lax.all_to_all(packed, 'cam', 0, 0)  12.4 us
    pallas_call x1, Pallas kernels, local(): pl.pallas_call(main_kernel, out_shape=jax.ShapeDtypeStruct((2 * N_CAM, RO...  2.34 us
    pallas_call x1, Pallas kernels, local(): pl.pallas_call(last_kernel, out_shape=(jax.ShapeDtypeStruct((36, PAIR_DEV...  1.06 us
    pallas_call x1, Pallas kernels, local(): pl.pallas_call(first_kernel, out_shape=(jax.ShapeDtypeStruct((N_CAM, 96,...  1.02 us
    convert_element_type x1, other arithmetic, local(): packed = ((rows(cam_jac, 0) + rows(pt_jac, 16)).astype(F32) + (cam + pt)....  0.9 us
  transfers between devices with their start and end apart: 1, of which 0 were waited for; matrix products, arithmetic and copies ran while one was open for 0% of the time, Pallas kernels for 3%

profile of v6, /device:TPU:64, one launch (start us, length us, event | category | flops | bytes accessed | tf_op | source)
XLA Modules:
  0.0 40.5 jit_solution(14418200207042694941)
XLA Ops:
  0.6 0.9 %fusion.1 = bf16[24,512]{1,0:T(8,128)(2,1)S(1)} fusion(f32[2,512]{1,0:T(2,128)} %param.9, s32[512]{0:T(512)} %param.11, s32[24]{0:T(128)S(1)} %iota_multiply_fusion, s32[512]{0:T(512)} %param.10, bf16[6,512]{1,0:T(8,128)(2,1)} %param.8, bf16[12,512]{1,0:T(8,128)(2,1)} %param.7), kind=kLoop, calls=%fused_computation.2 | loop fusion | flops 282624 | bytes 51296 | tf_op jit(solution)/shard_map/convert_element_type | solution.py:246
  1.6 12.4 %all_to_all.10.gat_ref.gat0_ref = bf16[8,24,512]{2,1,0:T(8,128)(2,1)S(1)} all-to-all(bf16[8,24,512]{2,1,0:T(8,128)(2,1)S(1)} %broadcast_in_dim.29), channel_id=1, replica_groups=mesh['cam'=8,'pts'=32] {'cam'}, dimensions={0} | all-to-all | bytes 393216 | tf_op jit(solution)/shard_map/all_to_all | solution.py:248
  14.0 0.0 copy-start
  14.0 0.0 collective-permute-start
  14.6 0.0 copy-done
  14.7 1.0 %shard_map.86 = (bf16[8,96,384]{2,1,0:T(8,128)(2,1)S(1)}, f32[32,128]{1,0:T(8,128)S(1)}, s32[2,64]{1,0:T(2,128)S(1)}) custom-call(bf16[8,24,512]{2,1,0:T(8,128)(2,1)S(1)} %all_to_all.10.gat_ref.gat0_ref, s32[2,64]{1,0:T(2,128)S(1)} %copy-done), custom_call_target="tpu_custom_call" | custom-call | flops 1000000000 | bytes 1000000 | tf_op jit(solution)/shard_map/pallas_call | solution.py:250
  15.7 0.0 collective-permute-done.gat1_ref
  15.7 2.3 %shard_map.87 = f32[16,80,128]{2,1,0:T(8,128)S(1)} custom-call(f32[1,1]{1,0:T(1,128)} %bitcast.1.lam_ref, f32[32,128]{1,0:T(8,128)S(1)} %get-tuple-element.5.totals_ref, bf16[8,96,384]{2,1,0:T(8,128)(2,1)S(1)} %get-tuple-element.6.d0_ref, bf16[8,24,512]{2,1,0:T(8,128)(2,1)S(1)} %all_to_all.10.gat_ref.gat0_ref, ...), custom_call_target="tpu_custom_call" | custom-call | tf_op jit(solution)/shard_map/pallas_call | solution.py:262
  18.1 21.3 %all_to_all.11 = f16[16,80,128]{2,1,0:T(8,128)(2,1)S(1)} all-to-all(f16[16,80,128]{2,1,0:T(8,128)(2,1)S(1)} %convert_element_type.26), channel_id=1, replica_groups={{0,8,16,24,26,18,10,2,4,12,20,28,30,22,14,6},{7,15,23,31,29,21,13,5,3,1..., dimensions={0} | all-to-all | bytes 655360 | tf_op jit(solution)/shard_map/all_to_all | solution.py:271
  39.4 1.1 %shard_map.88 = (f32[36,64]{1,0:T(8,128)}, f32[6,32]{1,0:T(8,128)}) custom-call(f32[16,80,128]{2,1,0:T(8,128)S(1)} %convert_element_type.27.got_ref, s32[2,64]{1,0:T(2,128)S(1)} %get-tuple-element.7.pairs_ref), custom_call_target="tpu_custom_call" | custom-call | tf_op jit(solution)/shard_map/pallas_call | solution.py:272
  (4 shorter events, 0.1 us)
Async XLA Ops:
  14.0 0.7 %copy-start = (s32[2,64]{1,0:T(2,128)S(1)}, s32[2,64]{1,0:T(2,128)}, u32[]{:S(2)}) copy-start(s32[2,64]{1,0:T(2,128)} %pairs_ref.1) | copy-start | bytes 1540
  14.0 1.7 %collective-permute-start = (bf16[8,24,512]{2,1,0:T(8,128)(2,1)S(1)}, bf16[8,24,512]{2,1,0:T(8,128)(2,1)S(1)}, u32[]{:S(2)}, u32[]{:S(2)}) collective-permute-start(bf16[8,24,512]{2,1,0:T(8,128)(2,1)S(1)} %all_to_all.10.gat_ref.gat0_ref), channel_id=1, source_target_pairs={{0,1},{1,0},{2,3},{3,2},{4,5},{5,4},{6,7},{7,6},{8,9},{9,8},{10,11... | collective-permute-start | bytes 589832 | tf_op jit(solution)/shard_map/ppermute | solution.py:249

commit v7 on v6

--- a/solution.py
+++ b/solution.py
@@ -16,7 +16,7 @@
 F32 = jnp.float32
 BF16 = jnp.bfloat16
 UNROLL = 8
-ORDERS = ([4 * (y if z % 2 == 0 else 3 - y) + z for z in range(4) for y in range(4)], [4 * (y if z % 2 == 0 else 3 - y) + z for z in range(4) for y in range(4)][::-1], [4 * (y if z % 2 == 0 else 3 - y) + z for z in range(4) for y in range(4)][::-1], [4 * (y if z % 2 == 0 else 3 - y) + z for z in range(4) for y in range(4)])
+ORDERS = ([4 * ((k + 0) % 4) + (k // 4 + 0) % 4 for k in range(16)], [4 * ((k + 2) % 4) + (k // 4 + 2) % 4 for k in range(16)], [4 * ((k + 1) % 4) + (k // 4 + 1) % 4 for k in range(16)], [4 * ((k + 3) % 4) + (k // 4 + 3) % 4 for k in range(16)])
 SMALL = pltpu.CompilerParams(vmem_limit_bytes=16 * 1024 * 1024)
 SCRATCH = [pltpu.VMEM((N_CAM, 96, 384), BF16), pltpu.VMEM((2, 192, 384), BF16)]
 
@@ -106,13 +106,18 @@
     return pj[6:7] - half * 16.0, cell_hot
 
 
-def build_range(gat_ref, d_ref):
+def place(group, core):
+    at = jnp.where(group % 2 == 0, group // 2, N_CAM - 1 - group // 2)
+    return jnp.where(core == 0, at, N_CAM - 1 - at)
+
+
+def build_range(gat_ref, d_ref, owner):
     core = lax.axis_index("pts") % 2
     first = (lax.broadcasted_iota(jnp.int32, (SLICE, OBS_DEV), 0) + core * SLICE).astype(F32)
     iotac = lax.broadcasted_iota(jnp.int32, (2 * PT_DEV, OBS_DEV), 0).astype(F32)
 
     def one_group(g, totals):
-        x0, x1, pj = unpack(gat_ref[g])
+        x0, x1, pj = unpack(gat_ref[place(g, owner)])
         low, cell_hot = cells(pj, iotac)
         hot = jnp.where(first == low, 1.0, 0.0)
         left = spread(x0, x1, pj, [hot]) + stat_rows(x0, x1, pj)
@@ -128,7 +133,7 @@
 
 def first_kernel(gat_ref, pairs_ref, d_ref, totals_ref, near_ref):
     near_ref[...] = pairs_ref[...]
-    totals_ref[...] = build_range(gat_ref, d_ref)
+    totals_ref[...] = build_range(gat_ref, d_ref, lax.axis_index("pts") % 2)
 
 
 def fit(x):
@@ -139,11 +144,12 @@
 
 def main_kernel(lam_ref, totals_ref, d0_ref, gat0_ref, gat1_ref, out_ref, d1_ref, w_ref):
     group = lax.axis_index("cam")
-    turn = (group % 2) * 2 + lax.axis_index("pts") % 2
+    core = lax.axis_index("pts") % 2
+    turn = (group % 2) * 2 + core
     gat_refs = (gat0_ref, gat1_ref)
     iota16 = lax.broadcasted_iota(jnp.int32, (16, OBS_DEV), 0).astype(F32)
     iotac = lax.broadcasted_iota(jnp.int32, (2 * PT_DEV, OBS_DEV), 0).astype(F32)
-    totals = jnp.concatenate([totals_ref[...], build_range(gat1_ref, d1_ref)], axis=1)
+    totals = jnp.concatenate([totals_ref[...], build_range(gat1_ref, d1_ref, 1 - core)], axis=1)
     eight = totals[:8] + totals[8:16] + totals[16:24]
     ninth = totals[24:25] + totals[25:26] + totals[26:27]
     full, y = point_inverse([eight[i : i + 1] for i in range(8)] + [ninth], lam_ref[...])
@@ -151,7 +157,7 @@
     rhs = jnp.zeros((8, CAM_DEV), F32)
     for r in range(2):
         mine = slice(r * PT_DEV, (r + 1) * PT_DEV)
-        x0, x1, pj = unpack(gat_refs[r][group])
+        x0, x1, pj = unpack(gat_refs[r][place(group, core if r == 0 else 1 - core)])
         low, cell_hot = cells(pj, iotac)
         hot = jnp.where(iota16 == low, 1.0, 0.0)
         left = jnp.concatenate(spread(x0, x1, pj, [hot]), axis=0).astype(BF16)
@@ -245,7 +251,9 @@
     packed = ((rows(cam_jac, 0) + rows(pt_jac, 16)).astype(F32) + (cam + pt).astype(F32) + rows(resid, 12)
               + (second - lax.reduce_precision(second, 8, 7))).astype(BF16)
     packed = jnp.broadcast_to(packed[None], (N_CAM, 24, OBS_DEV))
-    gathered = lax.all_to_all(packed, "cam", 0, 0)
+    ring = [0, 2, 4, 6, 7, 5, 3, 1]
+    rings = [[g * N_PTS + p for g in (ring if p % 2 == 0 else ring[::-1])] for p in range(N_PTS)]
+    gathered = lax.all_to_all(packed, ("cam", "pts"), 0, 0, axis_index_groups=rings)
     other = lax.ppermute(gathered, "pts", [(i, i ^ 1) for i in range(N_PTS)])
     d0, totals, near = pl.pallas_call(
         first_kernel,

time: 40.7 us -> 40.2 us (0.988)
  the two profiles are of different devices: /device:TPU:64 before, /device:TPU:2 now
where the time goes in v7:
time: 40.2 us; the launch traced here: 39.9 us
  blocking collectives  33.1 us (82%)
  Pallas kernels  4.43 us (11%)
  between operations  1.34 us (3%)
  other arithmetic  1 us (2%)
    all_to_all x1, blocking collectives, local(): lax.all_to_all(send.astype(jnp.float16), ('cam', 'pts'), 0, 0, axis_index...  21.6 us
    all_to_all x1, blocking collectives, local(): lax.all_to_all(packed, ('cam', 'pts'), 0, 0, axis_index_groups=rings)  11.5 us
    pallas_call x1, Pallas kernels, local(): pl.pallas_call(main_kernel, out_shape=jax.ShapeDtypeStruct((2 * N_CAM, RO...  2.35 us
    pallas_call x1, Pallas kernels, local(): pl.pallas_call(last_kernel, out_shape=(jax.ShapeDtypeStruct((36, PAIR_DEV...  1.06 us
    pallas_call x1, Pallas kernels, local(): pl.pallas_call(first_kernel, out_shape=(jax.ShapeDtypeStruct((N_CAM, 96,...  1.02 us
    convert_element_type x1, other arithmetic, local(): packed = ((rows(cam_jac, 0) + rows(pt_jac, 16)).astype(F32) + (cam + pt)....  0.9 us
  transfers between devices with their start and end apart: 1, of which 0 were waited for; matrix products, arithmetic and copies ran while one was open for 0% of the time, Pallas kernels for 3%

profile of v7, /device:TPU:2, one launch (start us, length us, event | category | flops | bytes accessed | tf_op | source)
XLA Modules:
  0.0 39.9 jit_solution(13582190248045013692)
XLA Ops:
  0.6 0.9 %fusion.1 = bf16[24,512]{1,0:T(8,128)(2,1)S(1)} fusion(f32[2,512]{1,0:T(2,128)} %param.9, s32[512]{0:T(512)} %param.11, s32[24]{0:T(128)S(1)} %iota_multiply_fusion, s32[512]{0:T(512)} %param.10, bf16[6,512]{1,0:T(8,128)(2,1)} %param.8, bf16[12,512]{1,0:T(8,128)(2,1)} %param.7), kind=kLoop, calls=%fused_computation.2 | loop fusion | flops 282624 | bytes 51296 | tf_op jit(solution)/shard_map/convert_element_type | solution.py:252
  1.6 11.5 %all_to_all.10.gat_ref.gat0_ref = bf16[8,24,512]{2,1,0:T(8,128)(2,1)S(1)} all-to-all(bf16[8,24,512]{2,1,0:T(8,128)(2,1)S(1)} %broadcast_in_dim.29), channel_id=1, replica_groups={{0,64,128,192,224,160,96,32},{33,97,161,225,193,129,65,1},{2,66,130,194..., dimensions={0} | all-to-all | bytes 393216 | tf_op jit(solution)/shard_map/all_to_all | solution.py:256
  13.0 0.0 copy-start
  13.1 0.0 collective-permute-start
  13.7 0.0 copy-done
  13.7 1.0 %shard_map.86 = (bf16[8,96,384]{2,1,0:T(8,128)(2,1)S(1)}, f32[32,128]{1,0:T(8,128)S(1)}, s32[2,64]{1,0:T(2,128)S(1)}) custom-call(bf16[8,24,512]{2,1,0:T(8,128)(2,1)S(1)} %all_to_all.10.gat_ref.gat0_ref, s32[2,64]{1,0:T(2,128)S(1)} %copy-done), custom_call_target="tpu_custom_call" | custom-call | flops 1000000000 | bytes 1000000 | tf_op jit(solution)/shard_map/pallas_call | solution.py:258
  14.8 0.0 collective-permute-done.gat1_ref
  14.8 2.4 %shard_map.87 = f32[16,80,128]{2,1,0:T(8,128)S(1)} custom-call(f32[1,1]{1,0:T(1,128)} %bitcast.1.lam_ref, f32[32,128]{1,0:T(8,128)S(1)} %get-tuple-element.5.totals_ref, bf16[8,96,384]{2,1,0:T(8,128)(2,1)S(1)} %get-tuple-element.6.d0_ref, bf16[8,24,512]{2,1,0:T(8,128)(2,1)S(1)} %all_to_all.10.gat_ref.gat0_ref, ...), custom_call_target="tpu_custom_call" | custom-call | tf_op jit(solution)/shard_map/pallas_call | solution.py:270
  17.2 21.6 %all_to_all.11 = f16[16,80,128]{2,1,0:T(8,128)(2,1)S(1)} all-to-all(f16[16,80,128]{2,1,0:T(8,128)(2,1)S(1)} %convert_element_type.26), channel_id=1, replica_groups={{0,8,16,24,2,10,18,26,4,12,20,28,6,14,22,30},{21,29,5,13,23,31,7,15,17,..., dimensions={0} | all-to-all | bytes 655360 | tf_op jit(solution)/shard_map/all_to_all | solution.py:279
  38.9 1.1 %shard_map.88 = (f32[36,64]{1,0:T(8,128)}, f32[6,32]{1,0:T(8,128)}) custom-call(f32[16,80,128]{2,1,0:T(8,128)S(1)} %convert_element_type.27.got_ref, s32[2,64]{1,0:T(2,128)S(1)} %get-tuple-element.7.pairs_ref), custom_call_target="tpu_custom_call" | custom-call | tf_op jit(solution)/shard_map/pallas_call | solution.py:280
  (4 shorter events, 0.1 us)
Async XLA Ops:
  13.0 0.7 %copy-start = (s32[2,64]{1,0:T(2,128)S(1)}, s32[2,64]{1,0:T(2,128)}, u32[]{:S(2)}) copy-start(s32[2,64]{1,0:T(2,128)} %pairs_ref.1) | copy-start | bytes 1540
  13.1 1.7 %collective-permute-start = (bf16[8,24,512]{2,1,0:T(8,128)(2,1)S(1)}, bf16[8,24,512]{2,1,0:T(8,128)(2,1)S(1)}, u32[]{:S(2)}, u32[]{:S(2)}) collective-permute-start(bf16[8,24,512]{2,1,0:T(8,128)(2,1)S(1)} %all_to_all.10.gat_ref.gat0_ref), channel_id=1, source_target_pairs={{0,1},{1,0},{2,3},{3,2},{4,5},{5,4},{6,7},{7,6},{8,9},{9,8},{10,11... | collective-permute-start | bytes 589832 | tf_op jit(solution)/shard_map/ppermute | solution.py:257

commit v8 on v7

--- a/solution.py
+++ b/solution.py
@@ -107,8 +107,7 @@
 
 
 def place(group, core):
-    at = jnp.where(group % 2 == 0, group // 2, N_CAM - 1 - group // 2)
-    return jnp.where(core == 0, at, N_CAM - 1 - at)
+    return (group + 4 * core) % N_CAM
 
 
 def build_range(gat_ref, d_ref, owner):
@@ -251,8 +250,8 @@
     packed = ((rows(cam_jac, 0) + rows(pt_jac, 16)).astype(F32) + (cam + pt).astype(F32) + rows(resid, 12)
               + (second - lax.reduce_precision(second, 8, 7))).astype(BF16)
     packed = jnp.broadcast_to(packed[None], (N_CAM, 24, OBS_DEV))
-    ring = [0, 2, 4, 6, 7, 5, 3, 1]
-    rings = [[g * N_PTS + p for g in (ring if p % 2 == 0 else ring[::-1])] for p in range(N_PTS)]
+    ring = list(range(N_CAM))
+    rings = [[g * N_PTS + p for g in (ring if p % 2 == 0 else ring[4:] + ring[:4])] for p in range(N_PTS)]
     gathered = lax.all_to_all(packed, ("cam", "pts"), 0, 0, axis_index_groups=rings)
     other = lax.ppermute(gathered, "pts", [(i, i ^ 1) for i in range(N_PTS)])
     d0, totals, near = pl.pallas_call(

time: 40.2 us -> 40 us (level)
  the two profiles are of different devices: /device:TPU:2 before, /device:TPU:32 now
where the time goes in v8:
time: 40 us; the launch traced here: 39.7 us
  blocking collectives  33 us (82%)
  Pallas kernels  4.39 us (11%)
  between operations  1.34 us (3%)
  other arithmetic  1 us (2%)
    all_to_all x1, blocking collectives, local(): lax.all_to_all(send.astype(jnp.float16), ('cam', 'pts'), 0, 0, axis_index...  21.6 us
    all_to_all x1, blocking collectives, local(): lax.all_to_all(packed, ('cam', 'pts'), 0, 0, axis_index_groups=rings)  11.3 us
    pallas_call x1, Pallas kernels, local(): pl.pallas_call(main_kernel, out_shape=jax.ShapeDtypeStruct((2 * N_CAM, RO...  2.33 us
    pallas_call x1, Pallas kernels, local(): pl.pallas_call(last_kernel, out_shape=(jax.ShapeDtypeStruct((36, PAIR_DEV...  1.06 us
    pallas_call x1, Pallas kernels, local(): pl.pallas_call(first_kernel, out_shape=(jax.ShapeDtypeStruct((N_CAM, 96,...  1.01 us
    convert_element_type x1, other arithmetic, local(): packed = ((rows(cam_jac, 0) + rows(pt_jac, 16)).astype(F32) + (cam + pt)....  0.9 us
  transfers between devices with their start and end apart: 1, of which 0 were waited for; matrix products, arithmetic and copies ran while one was open for 0% of the time, Pallas kernels for 3%

profile of v8, /device:TPU:32, one launch (start us, length us, event | category | flops | bytes accessed | tf_op | source)
XLA Modules:
  0.0 39.7 jit_solution(13438227050030421952)
XLA Ops:
  0.6 0.9 %fusion.1 = bf16[24,512]{1,0:T(8,128)(2,1)S(1)} fusion(f32[2,512]{1,0:T(2,128)} %param.9, s32[512]{0:T(512)} %param.11, s32[24]{0:T(128)S(1)} %iota_multiply_fusion, s32[512]{0:T(512)} %param.10, bf16[6,512]{1,0:T(8,128)(2,1)} %param.8, bf16[12,512]{1,0:T(8,128)(2,1)} %param.7), kind=kLoop, calls=%fused_computation.2 | loop fusion | flops 282624 | bytes 51296 | tf_op jit(solution)/shard_map/convert_element_type | solution.py:251
  1.6 11.3 %all_to_all.10.gat_ref.gat0_ref = bf16[8,24,512]{2,1,0:T(8,128)(2,1)S(1)} all-to-all(bf16[8,24,512]{2,1,0:T(8,128)(2,1)S(1)} %broadcast_in_dim.29), channel_id=1, replica_groups={{0,32,64,96,128,160,192,224},{129,161,193,225,1,33,65,97},{2,34,66,98,1..., dimensions={0} | all-to-all | bytes 393216 | tf_op jit(solution)/shard_map/all_to_all | solution.py:255
  12.9 0.0 copy-start
  12.9 0.0 collective-permute-start
  13.6 0.0 copy-done
  13.6 1.0 %shard_map.86 = (bf16[8,96,384]{2,1,0:T(8,128)(2,1)S(1)}, f32[32,128]{1,0:T(8,128)S(1)}, s32[2,64]{1,0:T(2,128)S(1)}) custom-call(bf16[8,24,512]{2,1,0:T(8,128)(2,1)S(1)} %all_to_all.10.gat_ref.gat0_ref, s32[2,64]{1,0:T(2,128)S(1)} %copy-done), custom_call_target="tpu_custom_call" | custom-call | flops 1000000000 | bytes 1000000 | tf_op jit(solution)/shard_map/pallas_call | solution.py:257
  14.6 0.0 collective-permute-done.gat1_ref
  14.6 2.3 %shard_map.87 = f32[16,80,128]{2,1,0:T(8,128)S(1)} custom-call(f32[1,1]{1,0:T(1,128)} %bitcast.1.lam_ref, f32[32,128]{1,0:T(8,128)S(1)} %get-tuple-element.5.totals_ref, bf16[8,96,384]{2,1,0:T(8,128)(2,1)S(1)} %get-tuple-element.6.d0_ref, bf16[8,24,512]{2,1,0:T(8,128)(2,1)S(1)} %all_to_all.10.gat_ref.gat0_ref, ...), custom_call_target="tpu_custom_call" | custom-call | tf_op jit(solution)/shard_map/pallas_call | solution.py:269
  17.0 21.6 %all_to_all.11 = f16[16,80,128]{2,1,0:T(8,128)(2,1)S(1)} all-to-all(f16[16,80,128]{2,1,0:T(8,128)(2,1)S(1)} %convert_element_type.26), channel_id=1, replica_groups={{0,8,16,24,2,10,18,26,4,12,20,28,6,14,22,30},{21,29,5,13,23,31,7,15,17,..., dimensions={0} | all-to-all | bytes 655360 | tf_op jit(solution)/shard_map/all_to_all | solution.py:278
  38.7 1.1 %shard_map.88 = (f32[36,64]{1,0:T(8,128)}, f32[6,32]{1,0:T(8,128)}) custom-call(f32[16,80,128]{2,1,0:T(8,128)S(1)} %convert_element_type.27.got_ref, s32[2,64]{1,0:T(2,128)S(1)} %get-tuple-element.7.pairs_ref), custom_call_target="tpu_custom_call" | custom-call | tf_op jit(solution)/shard_map/pallas_call | solution.py:279
  (4 shorter events, 0.1 us)
Async XLA Ops:
  12.9 0.7 %copy-start = (s32[2,64]{1,0:T(2,128)S(1)}, s32[2,64]{1,0:T(2,128)}, u32[]{:S(2)}) copy-start(s32[2,64]{1,0:T(2,128)} %pairs_ref.1) | copy-start | bytes 1540
  12.9 1.7 %collective-permute-start = (bf16[8,24,512]{2,1,0:T(8,128)(2,1)S(1)}, bf16[8,24,512]{2,1,0:T(8,128)(2,1)S(1)}, u32[]{:S(2)}, u32[]{:S(2)}) collective-permute-start(bf16[8,24,512]{2,1,0:T(8,128)(2,1)S(1)} %all_to_all.10.gat_ref.gat0_ref), channel_id=1, source_target_pairs={{0,1},{1,0},{2,3},{3,2},{4,5},{5,4},{6,7},{7,6},{8,9},{9,8},{10,11... | collective-permute-start | bytes 589832 | tf_op jit(solution)/shard_map/ppermute | solution.py:256

commit v9 on v8

--- a/solution.py
+++ b/solution.py
@@ -219,10 +219,11 @@
     pick = jnp.where(
         lax.broadcasted_iota(jnp.int32, (128, 256), 0) == lefts, 1.0, 0.0
     ).astype(BF16)
-    first = nn(jnp.concatenate(split3(total[:48]), axis=0).astype(BF16), pick)
-    second = nn(jnp.concatenate(split3(tail), axis=0).astype(BF16), pick[:, :128])
-    z = jnp.concatenate([first, second], axis=1)
-    z = z[:48] + z[48:96] + z[96:]
+    both = jnp.concatenate([total[:48], tail], axis=0)
+    high = both.astype(BF16)
+    low = (both - high.astype(F32)).astype(BF16)
+    z = nn(high, pick) + nn(low, pick)
+    z = jnp.concatenate([z[:48], z[48:, :128]], axis=1)
     keep = lax.broadcasted_iota(jnp.int32, (SLICE, 384), 0) == rights
     rows = [
         jnp.sum(jnp.where(keep, z[l * 8 : (l + 1) * 8], 0.0), axis=0, keepdims=True) for l in range(6)

time: 40 us -> 40 us (level)
  no operation moved by 1% of the time
where the time goes in v9:
time: 40 us; the launch traced here: 39.7 us
  blocking collectives  33 us (82%)
  Pallas kernels  4.36 us (11%)
  between operations  1.34 us (3%)
  other arithmetic  1 us (2%)
    all_to_all x1, blocking collectives, local(): lax.all_to_all(send.astype(jnp.float16), ('cam', 'pts'), 0, 0, axis_index...  21.6 us
    all_to_all x1, blocking collectives, local(): lax.all_to_all(packed, ('cam', 'pts'), 0, 0, axis_index_groups=rings)  11.3 us
    pallas_call x1, Pallas kernels, local(): pl.pallas_call(main_kernel, out_shape=jax.ShapeDtypeStruct((2 * N_CAM, RO...  2.33 us
    pallas_call x1, Pallas kernels, local(): pl.pallas_call(last_kernel, out_shape=(jax.ShapeDtypeStruct((36, PAIR_DEV...  1.03 us
    pallas_call x1, Pallas kernels, local(): pl.pallas_call(first_kernel, out_shape=(jax.ShapeDtypeStruct((N_CAM, 96,...  1.01 us
    convert_element_type x1, other arithmetic, local(): packed = ((rows(cam_jac, 0) + rows(pt_jac, 16)).astype(F32) + (cam + pt)....  0.9 us
  transfers between devices with their start and end apart: 1, of which 0 were waited for; matrix products, arithmetic and copies ran while one was open for 0% of the time, Pallas kernels for 3%

profile of v9, /device:TPU:32, one launch (start us, length us, event | category | flops | bytes accessed | tf_op | source)
XLA Modules:
  0.0 39.7 jit_solution(2225569997419035468)
XLA Ops:
  0.6 0.9 %fusion.1 = bf16[24,512]{1,0:T(8,128)(2,1)S(1)} fusion(f32[2,512]{1,0:T(2,128)} %param.9, s32[512]{0:T(512)} %param.11, s32[24]{0:T(128)S(1)} %iota_multiply_fusion, s32[512]{0:T(512)} %param.10, bf16[6,512]{1,0:T(8,128)(2,1)} %param.8, bf16[12,512]{1,0:T(8,128)(2,1)} %param.7), kind=kLoop, calls=%fused_computation.2 | loop fusion | flops 282624 | bytes 51296 | tf_op jit(solution)/shard_map/convert_element_type | solution.py:252
  1.6 11.3 %all_to_all.10.gat_ref.gat0_ref = bf16[8,24,512]{2,1,0:T(8,128)(2,1)S(1)} all-to-all(bf16[8,24,512]{2,1,0:T(8,128)(2,1)S(1)} %broadcast_in_dim.29), channel_id=1, replica_groups={{0,32,64,96,128,160,192,224},{129,161,193,225,1,33,65,97},{2,34,66,98,1..., dimensions={0} | all-to-all | bytes 393216 | tf_op jit(solution)/shard_map/all_to_all | solution.py:256
  12.9 0.0 copy-start
  12.9 0.0 collective-permute-start
  13.6 0.0 copy-done
  13.6 1.0 %shard_map.86 = (bf16[8,96,384]{2,1,0:T(8,128)(2,1)S(1)}, f32[32,128]{1,0:T(8,128)S(1)}, s32[2,64]{1,0:T(2,128)S(1)}) custom-call(bf16[8,24,512]{2,1,0:T(8,128)(2,1)S(1)} %all_to_all.10.gat_ref.gat0_ref, s32[2,64]{1,0:T(2,128)S(1)} %copy-done), custom_call_target="tpu_custom_call" | custom-call | flops 1000000000 | bytes 1000000 | tf_op jit(solution)/shard_map/pallas_call | solution.py:258
  14.6 0.0 collective-permute-done.gat1_ref
  14.6 2.3 %shard_map.87 = f32[16,80,128]{2,1,0:T(8,128)S(1)} custom-call(f32[1,1]{1,0:T(1,128)} %bitcast.1.lam_ref, f32[32,128]{1,0:T(8,128)S(1)} %get-tuple-element.5.totals_ref, bf16[8,96,384]{2,1,0:T(8,128)(2,1)S(1)} %get-tuple-element.6.d0_ref, bf16[8,24,512]{2,1,0:T(8,128)(2,1)S(1)} %all_to_all.10.gat_ref.gat0_ref, ...), custom_call_target="tpu_custom_call" | custom-call | tf_op jit(solution)/shard_map/pallas_call | solution.py:270
  17.0 21.6 %all_to_all.11 = f16[16,80,128]{2,1,0:T(8,128)(2,1)S(1)} all-to-all(f16[16,80,128]{2,1,0:T(8,128)(2,1)S(1)} %convert_element_type.26), channel_id=1, replica_groups={{0,8,16,24,2,10,18,26,4,12,20,28,6,14,22,30},{21,29,5,13,23,31,7,15,17,..., dimensions={0} | all-to-all | bytes 655360 | tf_op jit(solution)/shard_map/all_to_all | solution.py:279
  38.7 1.0 %shard_map.88 = (f32[36,64]{1,0:T(8,128)}, f32[6,32]{1,0:T(8,128)}) custom-call(f32[16,80,128]{2,1,0:T(8,128)S(1)} %convert_element_type.27.got_ref, s32[2,64]{1,0:T(2,128)S(1)} %get-tuple-element.7.pairs_ref), custom_call_target="tpu_custom_call" | custom-call | tf_op jit(solution)/shard_map/pallas_call | solution.py:280
  (4 shorter events, 0.1 us)
Async XLA Ops:
  12.9 0.7 %copy-start = (s32[2,64]{1,0:T(2,128)S(1)}, s32[2,64]{1,0:T(2,128)}, u32[]{:S(2)}) copy-start(s32[2,64]{1,0:T(2,128)} %pairs_ref.1) | copy-start | bytes 1540
  12.9 1.7 %collective-permute-start = (bf16[8,24,512]{2,1,0:T(8,128)(2,1)S(1)}, bf16[8,24,512]{2,1,0:T(8,128)(2,1)S(1)}, u32[]{:S(2)}, u32[]{:S(2)}) collective-permute-start(bf16[8,24,512]{2,1,0:T(8,128)(2,1)S(1)} %all_to_all.10.gat_ref.gat0_ref), channel_id=1, source_target_pairs={{0,1},{1,0},{2,3},{3,2},{4,5},{5,4},{6,7},{7,6},{8,9},{9,8},{10,11... | collective-permute-start | bytes 589832 | tf_op jit(solution)/shard_map/ppermute | solution.py:257
